TPU v7x, 32 devices: a whole 2x2x4 slice. The times are simulated.
32 devices in a mesh: dp: 8 (over y, x, core), head: 4 (over z).
Axes of the slice: x: 2, y: 2, z: 4, core: 2. Of those that a mesh axis runs over, the one named last changes fastest.
Arguments:
- text_in: bfloat16 [4096, 768], P('dp'), may hold values from -6 to 6
- visual_in: bfloat16 [4096, 768], P('dp'), may hold values from -80 to 80
- visual_count: int32 [8], P('dp'), may hold values from 256 to 512, as said below
- line_index: int32 [2, 4096], P(None, 'dp'), may hold values from 0 to 47
- box_index: int32 [2, 2, 4096], P(None, None, 'dp'), may hold values from 0 to 31
- qkv_weight: bfloat16 [768, 3, 1536], P(None, None, 'head'), may hold values from -0.21875 to 0.21875
- bias_table: float32 [24, 64], P('head'), may hold values from -5 to 5
- out_weight: bfloat16 [1536, 768], replicated, may hold values from -0.75 to 0.75
- out_bias: float32 [768], replicated, may hold values from -3 to 3
- norm1_gain: float32 [768], replicated, may hold values from 0.25 to 1.75
- norm1_shift: float32 [768], replicated, may hold values from -3 to 3
- ffn_weight_in: bfloat16 [768, 3072], replicated, may hold values from -0.21875 to 0.21875
- ffn_bias_in: float32 [3072], replicated, may hold values from -3 to 3
- ffn_weight_out: bfloat16 [3072, 768], replicated, may hold values from -0.109375 to 0.109375
- ffn_bias_out: float32 [768], replicated, may hold values from -3 to 3
- norm2_gain: float32 [768], replicated, may hold values from 0.25 to 1.75
- norm2_shift: float32 [768], replicated, may hold values from -3 to 3
- batch_gain: float32 [768], replicated, may hold values from 0.25 to 1.75
- batch_shift: float32 [768], replicated, may hold values from -3 to 3
- cotangent: bfloat16 [4096, 768], P('dp'), may hold values from -6 to 6
Outputs:
- layer_out: bfloat16 [4096, 768], P('dp')
- grad_text: float32 [4096, 768], P(('dp', 'head'))
- grad_visual: float32 [4096, 768], P(('dp', 'head'))
- grad_qkv: float32 [768, 3, 1536], P('dp', None, 'head')
- grad_bias_table: float32 [24, 64], P('head', 'dp')
- grad_out_weight: float32 [1536, 768], P('head', 'dp')
- grad_out_bias: float32 [768], P(('dp', 'head'))
- grad_norm1_gain: float32 [768], P(('dp', 'head'))
- grad_norm1_shift: float32 [768], P(('dp', 'head'))
- grad_ffn_in: float32 [768, 3072], P(('dp', 'head'))
- grad_ffn_bias_in: float32 [3072], P(('dp', 'head'))
- grad_ffn_out: float32 [3072, 768], P(('dp', 'head'))
- grad_ffn_bias_out: float32 [768], P(('dp', 'head'))
- grad_norm2_gain: float32 [768], P(('dp', 'head'))
- grad_norm2_shift: float32 [768], P(('dp', 'head'))
- batch_gain_gradient: float32 [768], replicated
- batch_shift_gradient: float32 [768], replicated
Inputs may be any that keep to these rules, and one draw needn't show every extreme that they name: `visual_count`: each page holds half of 512 or 512 visual tokens; both occur in every draw.
All inputs are finite; a program needn't handle non-finite values.
Results may differ from a plain program's by a relative error of at most 0.018.
The roundings to bfloat16 on the way count: a program that leaves them out, or rounds other values in their place, can miss the bound.
Values may be sent and summed in bfloat16 or wider, within the bound.
No kernel may reach another device: no remote copies, remote signals or barrier semaphores. Data moves between devices by JAX's collectives and lax.ppermute only.
A program may use at most 128 MiB of HBM per device.

v0:
```python
import jax
import jax.numpy as jnp
from jax import lax
from jax.sharding import PartitionSpec as P

H = 12
HD = 64
NB_REL = 32
NB_BOX = 16
LINES = 48
BOXES = 32


EPSILON = 1e-05
FLOOR_SCORE = -1000000000.0
HIGHEST = lax.Precision.HIGHEST


def as_sent(x):
    return jax.tree.map(lambda a: a.astype(jnp.bfloat16) if a.dtype == jnp.float32 else a, x)


def layer_stats(hidden, gain, shift):
    average = jnp.mean(hidden, axis=-1, keepdims=True)
    centered_values = hidden - average
    scale_row = lax.rsqrt(
        jnp.mean(centered_values * centered_values, axis=-1, keepdims=True) + EPSILON
    )
    normal_hat = centered_values * scale_row
    return (normal_hat * gain + shift, normal_hat, scale_row)


def layer_back(upstream, normal_hat, scale_row, gain):
    scaled = upstream * gain
    return scale_row * (
        scaled
        - jnp.mean(scaled, axis=-1, keepdims=True)
        - normal_hat * jnp.mean(scaled * normal_hat, axis=-1, keepdims=True)
    )


def inner_rows(left, right):
    return lax.dot_general(
        left, right, (((0,), (0,)), ((), ())), preferred_element_type=jnp.float32
    )


def level_buckets(levels, half, offset, table_width):
    levels_iota = jnp.arange(levels, dtype=jnp.int32)
    offsets = levels_iota[None, :] - levels_iota[:, None]
    bucket = jnp.clip(offsets, -half, half - 1) + half + offset
    return (
        (bucket[:, :, None] == jnp.arange(table_width, dtype=jnp.int32)[None, None, :])
        .astype(jnp.float32)
        .reshape(levels * levels, table_width)
    )


def level_bias(table_rows, index_row, levels, half, offset):
    table_width = table_rows.shape[1]
    levels_iota = jnp.arange(levels, dtype=jnp.int32)
    one_hot = (index_row[:, None] == levels_iota[None, :]).astype(jnp.float32)
    bucket_map = level_buckets(levels, half, offset, table_width)
    pair_table = lax.dot_general(
        table_rows,
        bucket_map,
        (((1,), (1,)), ((), ())),
        precision=HIGHEST,
        preferred_element_type=jnp.float32,
    ).reshape(table_rows.shape[0], levels, levels)
    left_side = jnp.einsum(
        "il,hlm->him", one_hot, pair_table, precision=HIGHEST, preferred_element_type=jnp.float32
    )
    return jnp.einsum(
        "him,jm->hij", left_side, one_hot, precision=HIGHEST, preferred_element_type=jnp.float32
    )


def level_gradient(dscore, index_row, levels, half, offset, table_width):
    levels_iota = jnp.arange(levels, dtype=jnp.int32)
    one_hot = (index_row[:, None] == levels_iota[None, :]).astype(jnp.bfloat16)
    folded = jnp.einsum("hij,il->hlj", dscore, one_hot, preferred_element_type=jnp.float32)
    paired = jnp.einsum(
        "hlj,jm->hlm",
        folded,
        one_hot.astype(jnp.float32),
        precision=HIGHEST,
        preferred_element_type=jnp.float32,
    )
    bucket_map = level_buckets(levels, half, offset, table_width)
    return jnp.dot(
        paired.reshape(paired.shape[0], levels * levels),
        bucket_map,
        precision=HIGHEST,
        preferred_element_type=jnp.float32,
    )


def page_scores(query, key_rows, table_rows, line_row, box_rows, count, is_visual):
    bias = level_bias(table_rows, line_row, LINES, NB_REL // 2, 0)
    bias = bias + level_bias(table_rows, box_rows[0], BOXES, NB_BOX // 2, NB_REL)
    bias = bias + level_bias(table_rows, box_rows[1], BOXES, NB_BOX // 2, NB_REL + NB_BOX)
    scores = (
        jnp.einsum("ihd,jhd->hij", query, key_rows, preferred_element_type=jnp.float32)
        * HD ** (-0.5)
        + bias
    )
    position = jnp.arange(line_row.shape[0], dtype=jnp.int32)
    allowed = jnp.logical_or(jnp.logical_not(is_visual), position < count)
    scores = jnp.where(allowed[None, None, :], scores, FLOOR_SCORE)
    return (scores, allowed)


def per_device(
    text_in,
    visual_in,
    visual_count,
    line_index,
    box_index,
    qkv_weight,
    bias_table,
    out_weight,
    out_bias,
    norm1_gain,
    norm1_shift,
    ffn_weight_in,
    ffn_bias_in,
    ffn_weight_out,
    ffn_bias_out,
    norm2_gain,
    norm2_shift,
    batch_gain,
    batch_shift,
    cotangent,
):
    tok_rows, width = text_in.shape
    pages = visual_count.shape[0]
    page_len = tok_rows // pages
    local_width = qkv_weight.shape[2]
    heads_local = local_width // HD
    head_count = lax.axis_size("head")
    head_rank = lax.axis_index("head")
    is_visual = head_rank * heads_local >= H
    stream = is_visual.astype(jnp.int32)
    local_portion = tok_rows // head_count
    leading_row = head_rank * local_portion
    slots = jnp.arange(page_len, dtype=jnp.int32)
    valid_rows = (slots[None, :] < visual_count[:, None]).astype(jnp.float32).reshape(tok_rows, 1)
    visual = visual_in.astype(jnp.float32)
    feature_sum, total_count = lax.psum(
        (jnp.sum(visual * valid_rows, axis=0), jnp.sum(valid_rows)), "dp"
    )
    feature_mean = feature_sum / total_count
    centered_values = (visual - feature_mean) * valid_rows
    feature_var = lax.psum(jnp.sum(centered_values * centered_values, axis=0), "dp") / total_count
    batch_norm_scale = lax.rsqrt(feature_var + EPSILON)
    normed = ((centered_values * batch_norm_scale * batch_gain + batch_shift) * valid_rows).astype(
        jnp.bfloat16
    )
    stream_in = jnp.where(is_visual, normed, text_in)
    weight_flat = qkv_weight.reshape(width, 3 * local_width)
    qkv_rows = jnp.dot(stream_in, weight_flat, preferred_element_type=jnp.float32).astype(
        jnp.bfloat16
    )
    qkv_pages = qkv_rows.reshape(pages, page_len, 3, heads_local, HD)
    line_pages = lax.dynamic_index_in_dim(line_index, stream, 0, keepdims=False).reshape(
        pages, page_len
    )
    box_pages = jnp.transpose(
        lax.dynamic_index_in_dim(box_index, stream, 0, keepdims=False).reshape(2, pages, page_len),
        (1, 0, 2),
    )

    def forward_page(carry, inputs):
        qkv_page, line_row, box_rows, count = inputs
        scores, allowed = page_scores(
            qkv_page[:, 0], qkv_page[:, 1], bias_table, line_row, box_rows, count, is_visual
        )
        row_max = jnp.max(scores, axis=-1, keepdims=True)
        shifted_exp = jnp.exp(scores - row_max)
        row_total = jnp.sum(shifted_exp, axis=-1, keepdims=True)
        prob_low = (shifted_exp / row_total).astype(jnp.bfloat16)
        heads = jnp.einsum(
            "hij,jhd->ihd", prob_low, qkv_page[:, 2], preferred_element_type=jnp.float32
        )
        heads = heads * allowed[:, None, None].astype(jnp.float32)
        return (carry, (heads.astype(jnp.bfloat16), row_max[..., 0] + jnp.log(row_total[..., 0])))

    unused_carry, (head_pages, log_totals) = lax.scan(
        forward_page, jnp.zeros((), jnp.float32), (qkv_pages, line_pages, box_pages, visual_count)
    )
    heads_out = head_pages.reshape(tok_rows, local_width)
    attention = jnp.dot(
        lax.all_gather(heads_out, "head", axis=1, tiled=True),
        out_weight,
        preferred_element_type=jnp.float32,
    )
    hidden_one = text_in.astype(jnp.float32) + attention + out_bias
    after_one, hat_one, scale_one = layer_stats(hidden_one, norm1_gain, norm1_shift)
    after_low = after_one.astype(jnp.bfloat16)
    pre = jnp.dot(after_low, ffn_weight_in, preferred_element_type=jnp.float32) + ffn_bias_in
    act = jax.nn.gelu(pre, approximate=False).astype(jnp.bfloat16)
    hidden_two = after_one + (
        jnp.dot(act, ffn_weight_out, preferred_element_type=jnp.float32) + ffn_bias_out
    )
    result, hat_two, scale_two = layer_stats(hidden_two, norm2_gain, norm2_shift)
    result_low = result.astype(jnp.bfloat16)
    upstream = cotangent.astype(jnp.float32)
    dh_two = layer_back(upstream, hat_two, scale_two, norm2_gain)
    dbranch = dh_two.astype(jnp.bfloat16)
    dact = lax.dot_general(
        dbranch, ffn_weight_out, (((1,), (1,)), ((), ())), preferred_element_type=jnp.float32
    )
    gelu_pull = jax.vjp(lambda value: jax.nn.gelu(value, approximate=False), pre)[1]
    dpre = gelu_pull(dact)[0].astype(jnp.bfloat16)
    dy_one = dh_two + lax.dot_general(
        dpre, ffn_weight_in, (((1,), (1,)), ((), ())), preferred_element_type=jnp.float32
    )
    dh_one = layer_back(dy_one, hat_one, scale_one, norm1_gain)
    dmix = dh_one.astype(jnp.bfloat16)
    own_rows = lax.dynamic_slice_in_dim(out_weight, head_rank * local_width, local_width, 0)
    dheads = lax.dot_general(
        dmix, own_rows, (((1,), (1,)), ((), ())), preferred_element_type=jnp.float32
    ).astype(jnp.bfloat16)
    dh_share = lax.dynamic_slice_in_dim(dh_one, leading_row, local_portion, 0)
    summed = jax.tree.map(
        lambda part: part.astype(jnp.float32),
        lax.psum_scatter(
            as_sent(
                (
                    jnp.sum(dh_one, axis=0),
                    jnp.sum(dy_one * hat_one, axis=0),
                    jnp.sum(dy_one, axis=0),
                    inner_rows(after_low, dpre),
                    jnp.sum(dpre, axis=0, dtype=jnp.float32),
                    inner_rows(act, dbranch),
                    jnp.sum(dbranch, axis=0, dtype=jnp.float32),
                    jnp.sum(upstream * hat_two, axis=0),
                    jnp.sum(upstream, axis=0),
                )
            ),
            "dp",
            scatter_dimension=0,
            tiled=True,
        ),
    )
    ffn_grads = tuple(
        (
            lax.dynamic_slice_in_dim(
                piece, head_rank * (piece.shape[0] // head_count), piece.shape[0] // head_count, 0
            )
            for piece in summed
        )
    )
    grad_out_local = inner_rows(heads_out, dmix)
    dhead_pages = dheads.reshape(pages, page_len, heads_local, HD)
    table_width = bias_table.shape[1]

    def backward_page(table_grad, inputs):
        qkv_page, line_row, box_rows, count, log_total, dhead_page = inputs
        scores, allowed = page_scores(
            qkv_page[:, 0], qkv_page[:, 1], bias_table, line_row, box_rows, count, is_visual
        )
        prob = jnp.exp(scores - log_total[..., None])
        prob_low = prob.astype(jnp.bfloat16)
        dhead_page = dhead_page * allowed[:, None, None].astype(jnp.bfloat16)
        dvalue = jnp.einsum(
            "hij,ihd->jhd", prob_low, dhead_page, preferred_element_type=jnp.float32
        )
        dprob = jnp.einsum(
            "ihd,jhd->hij", dhead_page, qkv_page[:, 2], preferred_element_type=jnp.float32
        )
        inner = jnp.sum(prob * dprob, axis=-1, keepdims=True)
        dscore = (prob * (dprob - inner)).astype(jnp.bfloat16)
        dquery = jnp.einsum(
            "hij,jhd->ihd", dscore, qkv_page[:, 1], preferred_element_type=jnp.float32
        ) * HD ** (-0.5)
        dkey = jnp.einsum(
            "hij,ihd->jhd", dscore, qkv_page[:, 0], preferred_element_type=jnp.float32
        ) * HD ** (-0.5)
        table_grad = table_grad + level_gradient(
            dscore, line_row, LINES, NB_REL // 2, 0, table_width
        )
        table_grad = table_grad + level_gradient(
            dscore, box_rows[0], BOXES, NB_BOX // 2, NB_REL, table_width
        )
        table_grad = table_grad + level_gradient(
            dscore, box_rows[1], BOXES, NB_BOX // 2, NB_REL + NB_BOX, table_width
        )
        dqkv_page = jnp.stack([dquery, dkey, dvalue], axis=1).astype(jnp.bfloat16)
        return (table_grad, dqkv_page)

    table_grad, dqkv_pages = lax.scan(
        backward_page,
        jnp.zeros((heads_local, table_width), jnp.float32),
        (qkv_pages, line_pages, box_pages, visual_count, log_totals, dhead_pages),
    )
    dqkv_flat = dqkv_pages.reshape(tok_rows, 3 * local_width)
    grad_qkv_local = inner_rows(stream_in, dqkv_flat).reshape(width, 3, local_width)
    grad_qkv, grad_out_weight, grad_bias_table = (
        lax.psum_scatter(
            grad_qkv_local.astype(jnp.bfloat16), "dp", scatter_dimension=0, tiled=True
        ).astype(jnp.float32),
        lax.psum_scatter(
            grad_out_local.astype(jnp.bfloat16), "dp", scatter_dimension=1, tiled=True
        ).astype(jnp.float32),
        lax.psum_scatter(
            table_grad.astype(jnp.bfloat16), "dp", scatter_dimension=1, tiled=True
        ).astype(jnp.float32),
    )
    part_rows = lax.dot_general(
        dqkv_flat, weight_flat, (((1,), (1,)), ((), ())), preferred_element_type=jnp.float32
    )
    zero_rows = jnp.zeros_like(part_rows)
    input_sums = lax.psum_scatter(
        jnp.concatenate(
            [
                jnp.where(is_visual, zero_rows, part_rows),
                jnp.where(is_visual, part_rows, zero_rows),
            ],
            axis=1,
        ).astype(jnp.bfloat16),
        "head",
        scatter_dimension=0,
        tiled=True,
    ).astype(jnp.float32)
    grad_text = dh_share + input_sums[:, :width]
    valid_share = lax.dynamic_slice_in_dim(valid_rows, leading_row, local_portion, 0)
    normalized_portion = (
        lax.dynamic_slice_in_dim(centered_values, leading_row, local_portion, 0) * batch_norm_scale
    )
    normed_gradient = input_sums[:, width:] * valid_share
    batch_shift_gradient, batch_gain_gradient = lax.psum(
        (jnp.sum(normed_gradient, axis=0), jnp.sum(normed_gradient * normalized_portion, axis=0)),
        ("dp", "head"),
    )
    grad_visual = (
        valid_share
        * batch_norm_scale
        * batch_gain
        * (
            normed_gradient
            - batch_shift_gradient / total_count
            - normalized_portion * batch_gain_gradient / total_count
        )
    )
    (
        grad_out_bias,
        grad_norm1_gain,
        grad_norm1_shift,
        grad_ffn_in,
        grad_ffn_bias_in,
        grad_ffn_out,
        grad_ffn_bias_out,
        grad_norm2_gain,
        grad_norm2_shift,
    ) = ffn_grads
    return (
        result_low,
        grad_text,
        grad_visual,
        grad_qkv,
        grad_bias_table,
        grad_out_weight,
        grad_out_bias,
        grad_norm1_gain,
        grad_norm1_shift,
        grad_ffn_in,
        grad_ffn_bias_in,
        grad_ffn_out,
        grad_ffn_bias_out,
        grad_norm2_gain,
        grad_norm2_shift,
        batch_gain_gradient,
        batch_shift_gradient,
    )


def solution(mesh):
    in_specs = (
        P("dp", None),
        P("dp", None),
        P("dp"),
        P(None, "dp"),
        P(None, None, "dp"),
        P(None, None, "head"),
        P("head", None),
        P(),
        P(),
        P(),
        P(),
        P(),
        P(),
        P(),
        P(),
        P(),
        P(),
        P(),
        P(),
        P("dp", None),
    )
    out_specs = (
        P("dp", None),
        P(("dp", "head"), None),
        P(("dp", "head"), None),
        P("dp", None, "head"),
        P("head", "dp"),
        P("head", "dp"),
        P(("dp", "head")),
        P(("dp", "head")),
        P(("dp", "head")),
        P(("dp", "head"), None),
        P(("dp", "head")),
        P(("dp", "head"), None),
        P(("dp", "head")),
        P(("dp", "head")),
        P(("dp", "head")),
        P(),
        P(),
    )
    return jax.shard_map(
        per_device, mesh=mesh, in_specs=in_specs, out_specs=out_specs, check_vma=False
    )
```

profile of v0, /device:TPU:0, one launch (start us, length us, event | category | flops | bytes accessed | tf_op | source)
XLA Modules:
  0.0 417.6 jit_solution(16967327952835657942)
XLA Ops:
  7.4 1.3 convolution_bitcast_fusion.7
  9.5 2.5 convolution_bitcast_fusion
  13.3 4.7 %fusion.59 = f32[6,512,512]{1,2,0:T(8,128)} fusion(f32[6,512,48]{1,2,0:T(8,128)S(1)} %convolution_bitcast_fusion.1, s32[512]{0:T(512)S(1)} %bitcast.151), kind=kOutput, calls=%fused_computation.130 | convolution fusion | flops 905994240 | bytes 6883328 | tf_op jit(solution)/shard_map/while/body/eval_jaxpr/him,jm->hij/dot_general | solution.py:74
  19.2 4.6 %fusion.66 = f32[6,512,512]{1,2,0:T(8,128)} fusion(f32[6,512,32]{1,2,0:T(8,128)S(1)} %convolution_bitcast_fusion.4, s32[512]{0:T(512)S(1)} %bitcast.159), kind=kOutput, calls=%fused_computation.135 | convolution fusion | flops 603996160 | bytes 6686720 | tf_op jit(solution)/shard_map/while/body/eval_jaxpr/him,jm->hij/dot_general | solution.py:74
  23.8 3.9 copy.68
  29.2 16.2 %all-reduce.9 = (f32[768]{0:T(1024)S(1)}, f32[]{:T(128)}) all-reduce(f32[768]{0:T(1024)S(1)} %fusion.15, f32[]{:T(128)} %fusion.89), channel_id=1, replica_groups=mesh['dp'=8,'head'=4] {'dp'}, use_global_device_ids=true, to_apply=%region_1.0 | all-reduce | flops 769 | bytes 6152 | tf_op jit(solution)/shard_map/psum | solution.py:150
  46.1 1.5 fusion.16
  47.6 12.2 %psum.37 = f32[768]{0:T(1024)S(1)} all-reduce(f32[768]{0:T(1024)S(1)} %get-tuple-element.108), channel_id=1, replica_groups=mesh['dp'=8,'head'=4] {'dp'}, use_global_device_ids=true, to_apply=%region_5.0 | all-reduce | flops 768 | bytes 6144 | tf_op jit(solution)/shard_map/psum | solution.py:155
  61.2 4.3 %convolution_convert_fusion.2 = bf16[512,1152]{1,0:T(8,128)(2,1)} fusion(bf16[768,1152]{0,1:T(8,128)(2,1)} %bitcast.144, bf16[512,768]{1,0:T(8,128)(2,1)} %param.20, f32[768]{0:T(1024)S(1)} %copy-done.64, f32[768]{0:T(1024)S(1)} %copy-done.53, f32[768]{0:T(1024)S(1)} %add_rsqrt_fusion, f32[512]{0:T(512)S(1)} %fusion.92, pred[]{:T(512)S(6)} %ge.3, ...), kind=kOutput, calls=%fused_computation.31 | convolution fusion | flops 910098432 | bytes 4536321 | tf_op jit(solution)/shard_map/dot_general | solution.py:162
  65.5 1.6 copy.69
  69.1 8.2 %fusion.109 = (f32[6,512]{1,0:T(8,128)S(1)}, f32[6,512,512]{1,2,0:T(8,128)S(1)}) fusion(f32[6,512,32]{1,2,0:T(8,128)S(1)} %convolution_bitcast_fusion.3, s32[512]{0:T(512)S(1)} %bitcast.155, f32[6,512,512]{1,2,0:T(8,128)} %fusion.59, f32[6,512,512]{1,2,0:T(8,128)} %fusion.66, f32[6,512,512]{1,2,0:T(8,128)S(1)} %fusion.42, ...), kind=kOutput, calls=%fused_computation.192 | convolution fusion | flops 613430272 | bytes 25573888 | tf_op jit(solution)/shard_map/while/body/eval_jaxpr/him,jm->hij/dot_general | solution.py:74
  78.2 1.7 copy-done.1
  79.9 2.0 fusion.28
  82.9 35.4 %all-gather.2.cloned.1.call-done = bf16[512,1536]{0,1:T(8,128)(2,1)} async-done(((bf16[512,384]{0,1:T(8,128)(2,1)}), bf16[512,1536]{0,1:T(8,128)(2,1)}) %all-gather.2.cloned.1.call-update) | async-done | bytes 1572880 | tf_op jit(solution)/shard_map/all_gather | solution.py:194
  118.4 3.3 fusion.110
  122.1 19.6 %multiply_convert_fusion.1 = (bf16[512,3072]{1,0:T(8,128)(2,1)S(1)}, f32[512,3072]{1,0:T(8,128)}, f32[512,3072]{1,0:T(8,128)}) fusion(f32[3072]{0:T(1024)S(1)} %copy-done.61, bf16[768,3072]{1,0:T(8,128)(2,1)} %param.31, f32[512,768]{1,0:T(8,128)S(1)} %get-tuple-element.119, f32[768]{0:T(1024)S(1)} %copy-done.66, f32[768]{0:T(1024)S(1)} %copy-done.51, ...), kind=kOutput, calls=%fused_computation.6 | convolution fusion | flops 2521694208 | bytes 22042624 | tf_op jit(solution)/shard_map/dot_general | solution.py:201
  141.8 2.8 fusion.111
  145.0 2.1 fusion.20
  147.1 1.3 convert_reduce_fusion
  148.4 9.9 %fusion.112 = (bf16[3072]{0:T(1024)(128)(2,1)}, bf16[512,3072]{1,0:T(8,128)(2,1)S(1)}) fusion(f32[512,3072]{1,0:T(8,128)} %get-tuple-element.105, bf16[3072,768]{1,0:T(8,128)(2,1)} %param.33, f32[512,768]{1,0:T(8,128)S(1)} %get-tuple-element.99, f32[512,3072]{1,0:T(8,128)} %get-tuple-element.120, f32[3072]{0:T(1024)S(1)} %copy-done.61), kind=kOutput, calls=%fused_computation.195 | convolution fusion | flops 2441475072 | bytes 22038528 | tf_op jit(solution)/shard_map/dot_general | solution.py:211
  158.3 7.2 %multiply_reduce_fusion.1 = (bf16[768]{0:T(1024)(128)(2,1)}, f32[512]{0:T(512)S(1)}, f32[512]{0:T(512)S(1)}, bf16[768]{0:T(1024)(128)(2,1)}, f32[512,768]{1,0:T(8,128)S(1)}) fusion(f32[512,768]{1,0:T(8,128)S(1)} %get-tuple-element.119, f32[512]{0:T(512)S(1)} %add_rsqrt_fusion.2, f32[512]{0:T(512)S(1)} %broadcast_multiply_fusion.5, f32[768]{0:T(1024)S(1)} %copy-done.51, ...), kind=kOutput, calls=%fused_computation.48 | convolution fusion | flops 2419848704 | bytes 12597248 | tf_op jit(solution)/shard_map/dot_general | solution.py:216
  165.6 1.1 fusion.105
  167.3 4.1 multiply_reduce_fusion
  171.3 4.6 %multiply_convert_fusion = bf16[6,512,512]{1,2,0:T(8,128)(2,1)S(1)} fusion(f32[6,512,512]{1,2,0:T(8,128)} %get-tuple-element.125, f32[6,512,512]{1,2,0:T(8,128)S(1)} %bitcast.136, f32[6,512]{1,0:T(8,128)S(1)} %get-tuple-element.124, f32[6,512]{1,0:T(8,128)S(1)} %log_add_fusion), kind=kLoop, calls=%fused_computation.2 | loop fusion | flops 6291456 | bytes 15753216 | tf_op jit(solution)/shard_map/while/body/eval_jaxpr/convert_element_type | solution.py:274
  176.0 1.8 fusion.25
  177.8 1.4 fusion.26
  179.2 1.4 convolution_convert_fusion.4
  180.8 4.0 fusion.22
  185.0 1.1 copy-done.15
  186.0 2.8 convolution_convert_fusion.3
  188.9 3.1 select_convert_fusion.1
  192.1 1.3 pad_maximum_fusion
  193.7 7.4 %convolution_convert_fusion.1 = bf16[768,3072]{1,0:T(8,128)(2,1)} fusion(bf16[512,3072]{1,0:T(8,128)(2,1)} %copy-done.70, f32[512,768]{1,0:T(8,128)} %copy-done.5, f32[768]{0:T(1024)S(1)} %copy-done.67, f32[768]{0:T(1024)S(1)} %copy-done.52, f32[512]{0:T(512)S(1)} %copy-done.45, f32[512]{0:T(512)S(1)} %copy-done.36), kind=kOutput, calls=%fused_computation.25 | convolution fusion | flops 2420244480 | bytes 9447424 | tf_op jit(solution)/shard_map/dot_general | solution.py:43
  201.2 7.2 %convolution_convert_fusion = bf16[3072,768]{1,0:T(8,128)(2,1)} fusion(bf16[512,3072]{1,0:T(8,128)(2,1)} %copy-done.69, f32[512,768]{1,0:T(8,128)} %copy-done.12), kind=kOutput, calls=%fused_computation.24 | convolution fusion | flops 2418671616 | bytes 9437184 | tf_op jit(solution)/shard_map/dot_general | solution.py:43
  211.6 3.1 convolution_bitcast_fusion.2
  219.7 24.2 %all-reduce.10 = (bf16[6,64]{1,0:T(8,128)(2,1)S(1)}, bf16[768]{0:T(1024)(128)(2,1)S(1)}, bf16[768]{0:T(1024)(128)(2,1)S(1)}, bf16[768]{0:T(1024)(128)(2,1)S(1)},...) all-reduce(bf16[6,64]{1,0:T(8,128)(2,1)S(1)} %fusion.33, ...), channel_id=4, replica_groups=mesh['dp'=8,'head'=4] {'dp'}, use_global_device_ids=true, to_apply=%region_23.24.clone | all-reduce | flops 8064 | bytes 32256
  249.1 1.6 convert_element_type.256
  250.7 6.2 %reduce-scatter.9.cloned.1.call-done = bf16[96,3,384]{2,0,1:T(8,128)(2,1)} async-done(((bf16[768,3,384]{2,0,1:T(8,128)(2,1)}), bf16[96,3,384]{2,0,1:T(8,128)(2,1)}) %reduce-scatter.9.cloned.1.call-update) | async-done | bytes 221200 | tf_op jit(solution)/shard_map/reduce_scatter | solution.py:301
  256.9 1.7 convert_element_type.252
  258.6 35.7 %reduce-scatter.7.cloned.1.call-done = bf16[128,1536]{1,0:T(8,128)(2,1)} async-done(((bf16[512,1536]{1,0:T(8,128)(2,1)}), bf16[128,1536]{1,0:T(8,128)(2,1)}) %reduce-scatter.7.cloned.1.call-update) | async-done | bytes 393232 | tf_op jit(solution)/shard_map/reduce_scatter | solution.py:315
  294.3 1.1 convert_element_type.249
  295.4 1.1 fusion.45
  296.5 39.5 %all-reduce.8 = (f32[768]{0:T(1024)S(1)}, f32[768]{0:T(1024)S(1)}) all-reduce(f32[768]{0:T(1024)S(1)} %get-tuple-element.85, f32[768]{0:T(1024)S(1)} %get-tuple-element.84), channel_id=1, replica_groups=mesh['dp'=8,'head'=4] {'dp','head'}, use_global_device_ids=true, to_apply=%region_21.22 | all-reduce | flops 1536 | bytes 12288 | tf_op jit(solution)/shard_map/psum | solution.py:333
  336.7 2.8 subtract_multiply_fusion.3
  339.6 11.5 %reduce-scatter.13.cloned.1.call-done = bf16[96,3072]{1,0:T(8,128)(2,1)} async-done(((bf16[768,3072]{1,0:T(8,128)(2,1)}), bf16[96,3072]{1,0:T(8,128)(2,1)}) %reduce-scatter.13.cloned.1.call-update) | async-done | bytes 589840 | tf_op jit(solution)/shard_map/reduce_scatter | solution.py:228
  351.1 1.6 dynamic-slice_convert_fusion.1
  352.7 56.0 %reduce-scatter.15.cloned.1.call-done = bf16[384,768]{1,0:T(8,128)(2,1)} async-done(((bf16[3072,768]{1,0:T(8,128)(2,1)}), bf16[384,768]{1,0:T(8,128)(2,1)}) %reduce-scatter.15.cloned.1.call-update) | async-done | bytes 589840 | tf_op jit(solution)/shard_map/reduce_scatter | solution.py:228
  408.7 1.6 dynamic-slice_convert_fusion
  (225 shorter events, 24.1 us)
Async XLA Ops:
  7.2 111.1 %copy-start = (bf16[1536,768]{1,0:T(8,128)(2,1)S(1)}, bf16[1536,768]{1,0:T(8,128)(2,1)}, u32[]{:S(2)}) copy-start(bf16[1536,768]{1,0:T(8,128)(2,1)} %param.27) | copy-start | bytes 7077892
  7.2 111.1 %all-gather.2.cloned.1.call-start = ((), (), s32[]{:S(2)}) async-start(), calls=%async_computation.5 | async-start | bytes 1966080 | tf_op jit(solution)/shard_map/all_gather | solution.py:194
  7.3 10.6 %copy-start.24 = (s32[32,32]{1,0:T(8,128)}, s32[32,32]{1,0:T(8,128)S(1)}, u32[]{:S(2)}) copy-start(s32[32,32]{1,0:T(8,128)S(1)} %fusion.88) | copy-start | bytes 12292
  12.8 5.1 %copy-start.26 = (s32[1,512]{1,0:T(1,128)}, s32[1,512]{1,0:T(1,128)S(1)}, u32[]{:S(2)}) copy-start(s32[1,512]{1,0:T(1,128)S(1)} %constant_dynamic-slice_fusion.2) | copy-start | bytes 6148
  13.3 4.8 %copy-start.62 = (f32[6,64]{1,0:T(8,128)S(1)}, f32[6,64]{1,0:T(8,128)}, u32[]{:S(2)}) copy-start(f32[6,64]{1,0:T(8,128)} %param.26) | copy-start | bytes 4612
  13.3 5.3 %copy-start.60 = (s32[2,2,512]{2,1,0:T(2,128)S(1)}, s32[2,2,512]{2,1,0:T(2,128)}, u32[]{:S(2)}) copy-start(s32[2,2,512]{2,1,0:T(2,128)} %param.24) | copy-start | bytes 24580
  18.6 50.5 %copy-start.28 = (s32[1,1,512]{2,1,0:T(1,128)}, s32[1,1,512]{2,1,0:T(1,128)S(1)}, u32[]{:S(2)}) copy-start(s32[1,1,512]{2,1,0:T(1,128)S(1)} %get-tuple-element.114) | copy-start | bytes 6148
  23.8 5.2 %copy-start.8 = (bf16[512,768]{1,0:T(8,128)(2,1)S(1)}, bf16[512,768]{1,0:T(8,128)(2,1)}, u32[]{:S(2)}) copy-start(bf16[512,768]{1,0:T(8,128)(2,1)} %param.21) | copy-start | bytes 2359300
  23.8 37.4 %copy-start.53 = (f32[768]{0:T(1024)S(1)}, f32[768]{0:T(1024)}, u32[]{:S(2)}) copy-start(f32[768]{0:T(1024)} %param.37) | copy-start | bytes 9220
  23.8 37.4 %copy-start.64 = (f32[768]{0:T(1024)S(1)}, f32[768]{0:T(1024)}, u32[]{:S(2)}) copy-start(f32[768]{0:T(1024)} %param.38) | copy-start | bytes 9220
  28.4 32.2 %copy-start.37 = (f32[512]{0:T(512)}, f32[512]{0:T(512)S(1)}, u32[]{:S(2)}) copy-start(f32[512]{0:T(512)S(1)} %fusion.92) | copy-start | bytes 6148
  46.1 14.5 %copy-start.39 = (f32[768]{0:T(1024)}, f32[768]{0:T(1024)S(1)}, u32[]{:S(2)}) copy-start(f32[768]{0:T(1024)S(1)} %broadcast_divide_fusion.1) | copy-start | bytes 9220
  82.0 167.2 %reduce-scatter.11.cloned.1.call-start = ((), (), s32[]{:S(2)}) async-start(), calls=%async_computation.8 | async-start | bytes 663552 | tf_op jit(solution)/shard_map/reduce_scatter | solution.py:304
  118.3 3.7 copy-start.51
  118.3 3.7 copy-start.61
  118.3 3.7 copy-start.66
  118.3 23.4 %slice-start.2 = ((s8[4718592]{0:T(1024)(128)(4,1)}), s8[4194304]{0:T(1024)(128)(4,1)S(1)}, s32[]{:S(2)}) async-start(s8[4718592]{0:T(1024)(128)(4,1)} %bitcast.162), calls=%async_computation.13 | async-start | bytes 8388608
  121.7 43.9 %copy-start.5 = (f32[512,768]{1,0:T(8,128)}, f32[512,768]{1,0:T(8,128)S(1)}, u32[]{:S(2)}) copy-start(f32[512,768]{1,0:T(8,128)S(1)} %get-tuple-element.119) | copy-start | bytes 4718596
  121.7 43.8 %copy-start.35 = (f32[512]{0:T(512)}, f32[512]{0:T(512)S(1)}, u32[]{:S(2)}) copy-start(f32[512]{0:T(512)S(1)} %broadcast_multiply_fusion.5) | copy-start | bytes 6148
  122.1 43.5 %copy-start.44 = (f32[512]{0:T(512)}, f32[512]{0:T(512)S(1)}, u32[]{:S(2)}) copy-start(f32[512]{0:T(512)S(1)} %add_rsqrt_fusion.2) | copy-start | bytes 6148
  122.1 19.7 %slice-start.3 = ((s8[4718592]{0:T(1024)(128)(4,1)}), s8[524288]{0:T(1024)(128)(4,1)S(1)}, s32[]{:S(2)}) async-start(s8[4718592]{0:T(1024)(128)(4,1)} %bitcast.162), calls=%async_computation.14 | async-start | bytes 1048576
  122.1 19.7 %copy-start.63 = (f32[768]{0:T(1024)S(1)}, f32[768]{0:T(1024)}, u32[]{:S(2)}) copy-start(f32[768]{0:T(1024)} %param.34) | copy-start | bytes 9220
  147.1 20.1 %slice-start = ((s8[6291456]{0:T(1024)(128)(4,1)}), s8[4194304]{0:T(1024)(128)(4,1)S(1)}, s32[]{:S(2)}) async-start(s8[6291456]{0:T(1024)(128)(4,1)} %bitcast.135), calls=%async_computation.11 | async-start | bytes 8388608
  148.4 9.9 %copy-start.12 = (f32[512,768]{1,0:T(8,128)}, f32[512,768]{1,0:T(8,128)S(1)}, u32[]{:S(2)}) copy-start(f32[512,768]{1,0:T(8,128)S(1)} %get-tuple-element.99) | copy-start | bytes 4718596
  148.4 18.9 %slice-start.1 = ((s8[6291456]{0:T(1024)(128)(4,1)}), s8[2097152]{0:T(1024)(128)(4,1)S(1)}, s32[]{:S(2)}) async-start(s8[6291456]{0:T(1024)(128)(4,1)} %bitcast.135), calls=%async_computation.12 | async-start | bytes 4194304
  158.3 7.2 %copy-start.70 = (bf16[512,3072]{1,0:T(8,128)(2,1)}, bf16[512,3072]{1,0:T(8,128)(2,1)S(1)}, u32[]{:S(2)}) copy-start(bf16[512,3072]{1,0:T(8,128)(2,1)S(1)} %get-tuple-element.127) | copy-start | bytes 9437188
  166.7 12.5 %copy-start.4 = (f32[512,768]{1,0:T(8,128)}, f32[512,768]{1,0:T(8,128)S(1)}, u32[]{:S(2)}) copy-start(f32[512,768]{1,0:T(8,128)S(1)} %get-tuple-element.101) | copy-start | bytes 4718596
  167.2 4.1 copy-start.6
  180.6 5.4 %copy-start.9 = (bf16[512,768]{1,0:T(8,128)(2,1)S(1)}, bf16[512,768]{1,0:T(8,128)(2,1)}, u32[]{:S(2)}) copy-start(bf16[512,768]{1,0:T(8,128)(2,1)} %param.21) | copy-start | bytes 2359300
  180.6 76.2 %reduce-scatter.9.cloned.1.call-start = ((), (), s32[]{:S(2)}) async-start(), calls=%async_computation.7 | async-start | bytes 1990656 | tf_op jit(solution)/shard_map/reduce_scatter | solution.py:301
  180.7 4.1 copy-start.13
  180.7 4.1 copy-start.14
  180.7 5.3 %copy-start.16 = (bf16[512,768]{1,0:T(8,128)(2,1)S(1)}, bf16[512,768]{1,0:T(8,128)(2,1)}, u32[]{:S(2)}) copy-start(bf16[512,768]{1,0:T(8,128)(2,1)} %param.20) | copy-start | bytes 2359300
  180.7 5.3 %copy-start.33 = (f32[768]{0:T(1024)S(1)}, f32[768]{0:T(1024)}, u32[]{:S(2)}) copy-start(f32[768]{0:T(1024)} %copy-done.32) | copy-start | bytes 9220
  180.7 5.3 %copy-start.38 = (f32[512]{0:T(512)S(1)}, f32[512]{0:T(512)}, u32[]{:S(2)}) copy-start(f32[512]{0:T(512)} %copy-done.37) | copy-start | bytes 6148
  180.7 5.3 %copy-start.40 = (f32[768]{0:T(1024)S(1)}, f32[768]{0:T(1024)}, u32[]{:S(2)}) copy-start(f32[768]{0:T(1024)} %copy-done.39) | copy-start | bytes 9220
  180.8 5.3 %copy-start.54 = (f32[768]{0:T(1024)S(1)}, f32[768]{0:T(1024)}, u32[]{:S(2)}) copy-start(f32[768]{0:T(1024)} %param.37) | copy-start | bytes 9220
  180.8 5.3 %copy-start.65 = (f32[768]{0:T(1024)S(1)}, f32[768]{0:T(1024)}, u32[]{:S(2)}) copy-start(f32[768]{0:T(1024)} %param.38) | copy-start | bytes 9220
  188.9 105.4 %reduce-scatter.7.cloned.1.call-start = ((), (), s32[]{:S(2)}) async-start(), calls=%async_computation.6 | async-start | bytes 1966080 | tf_op jit(solution)/shard_map/reduce_scatter | solution.py:315
  193.4 157.7 %reduce-scatter.13.cloned.1.call-start = ((), (), s32[]{:S(2)}) async-start(), calls=%async_computation.9 | async-start | bytes 5308416 | tf_op jit(solution)/shard_map/reduce_scatter | solution.py:228
  201.1 207.6 %reduce-scatter.15.cloned.1.call-start = ((), (), s32[]{:S(2)}) async-start(), calls=%async_computation.10 | async-start | bytes 5308416 | tf_op jit(solution)/shard_map/reduce_scatter | solution.py:228
  208.4 6.7 %copy-start.20 = (s32[48,48]{1,0:T(8,128)S(1)}, s32[48,48]{1,0:T(8,128)}, u32[]{:S(2)}) copy-start(s32[48,48]{1,0:T(8,128)} %copy-done.19) | copy-start | bytes 27652
  208.4 7.6 %copy-start.31 = (s32[1,1,512]{2,1,0:T(1,128)S(1)}, s32[1,1,512]{2,1,0:T(1,128)}, u32[]{:S(2)}) copy-start(s32[1,1,512]{2,1,0:T(1,128)} %copy-done.30) | copy-start | bytes 6148
  211.6 4.4 %copy-start.3 = (bf16[6,512,512]{1,2,0:T(8,128)(2,1)S(1)}, bf16[6,512,512]{1,2,0:T(8,128)(2,1)}, u32[]{:S(2)}) copy-start(bf16[6,512,512]{1,2,0:T(8,128)(2,1)} %copy-done.2) | copy-start | bytes 9437188
  217.8 77.5 %copy-start.34 = (f32[768]{0:T(1024)S(1)}, f32[768]{0:T(1024)}, u32[]{:S(2)}) copy-start(f32[768]{0:T(1024)} %copy-done.32) | copy-start | bytes 9220
  217.8 118.9 %copy-start.55 = (f32[768]{0:T(1024)S(1)}, f32[768]{0:T(1024)}, u32[]{:S(2)}) copy-start(f32[768]{0:T(1024)} %param.37) | copy-start | bytes 9220
  336.0 74.3 %copy-start.56 = (f32[768]{0:T(1024)}, f32[768]{0:T(1024)S(1)}, u32[]{:S(2)}) copy-start(f32[768]{0:T(1024)S(1)} %get-tuple-element.86) | copy-start | bytes 9220
  336.0 74.3 %copy-start.57 = (f32[768]{0:T(1024)}, f32[768]{0:T(1024)S(1)}, u32[]{:S(2)}) copy-start(f32[768]{0:T(1024)S(1)} %get-tuple-element.87) | copy-start | bytes 9220
  (33 other events, 74.2 us)
Sparse Core Ops, SparseCore 0:
  82.1 36.2 all-gather.1
  180.7 33.2 reduce-scatter.10
  217.4 39.4 reduce-scatter.8
  259.0 35.2 reduce-scatter.6
  297.6 53.4 reduce-scatter.12
  354.8 53.8 reduce-scatter.14
where the time goes:
time: 423 us; the launch traced here: 418 us
  waiting for transfers between devices  145 us (34%)
  matrix products  115 us (27%)
  blocking collectives  92.1 us (22%)
  other arithmetic  30.6 us (7%)
  between operations  18.3 us (4%)
  local copies, waits for them, and re-layouts  16.6 us (4%)
    reduce_scatter x2, waiting for transfers between devices, per_device(): lax.psum_scatter(as_sent((jnp.sum(dh_one, axis=0), jnp.sum(dy_one * hat_o...  67.5 us
    psum x1, blocking collectives, per_device(): lax.psum((jnp.sum(normed_gradient, axis=0), jnp.sum(normed_gradient * nor...  39.5 us
    reduce_scatter x1, waiting for transfers between devices, per_device(): lax.psum_scatter(jnp.concatenate([jnp.where(is_visual, zero_rows, part_ro...  35.7 us
    all_gather x1, waiting for transfers between devices, per_device(): lax.all_gather(heads_out, 'head', axis=1, tiled=True)  35.4 us
    unnamed x1, blocking collectives  24.2 us
    dot_general x1, matrix products, per_device(): jnp.dot(after_low, ffn_weight_in, preferred_element_type=jnp.float32)  19.6 us
    dot_general x4, matrix products, inner_rows(): lax.dot_general(left, right, (((0,), (0,)), ((), ())), preferred_element_...  18.8 us
    dot_general x3, matrix products, level_bias(): jnp.einsum('him,jm->hij', left_side, one_hot, precision=HIGHEST, preferre...  17.4 us
  transfers between devices with their start and end apart: 6, of which 5 were waited for; matrix products, arithmetic and copies ran while one was open for 12% of the time, Pallas kernels for 0%

commit v1 on v0

v1 whole, which is shorter than its diff:
```python
import functools

import jax
import jax.numpy as jnp
from jax import lax
from jax.experimental import pallas as pl
from jax.experimental.pallas import tpu as pltpu
from jax.sharding import PartitionSpec as P

H = 12
HD = 64
NB_REL = 32
NB_BOX = 16
LINES = 48
BOXES = 32

EPSILON = 1e-05
FLOOR_SCORE = -1000000000.0
SCALE = HD ** (-0.5)
LEVELS = 128
MASK_LANE = LINES + 2 * BOXES
VMEM_LIMIT = 60 * 1024 * 1024

F32 = jnp.float32
BF16 = jnp.bfloat16

NN = (((1,), (0,)), ((), ()))
NT = (((1,), (1,)), ((), ()))
TN = (((0,), (0,)), ((), ()))


def dot(left, right, dims=NN):
    return lax.dot_general(left, right, dims, preferred_element_type=F32)


def iota(shape, axis):
    return lax.broadcasted_iota(jnp.int32, shape, axis)


def params():
    return pltpu.CompilerParams(vmem_limit_bytes=VMEM_LIMIT)


def vmem(count):
    return [pl.BlockSpec(memory_space=pltpu.VMEM)] * count


def stream_is_visual():
    return lax.axis_index("head") >= lax.axis_size("head") // 2


GROUPS = (
    (0, LINES, NB_REL // 2, 0),
    (LINES, LINES + BOXES, NB_BOX // 2, NB_REL),
    (LINES + BOXES, LINES + 2 * BOXES, NB_BOX // 2, NB_REL + NB_BOX),
)


def bucket_map(half, offset, table_width):
    level = iota((table_width, LEVELS), 1) - LEVELS // 2
    bucket = jnp.clip(level, -half, half - 1) + half + offset
    return (bucket == iota((table_width, LEVELS), 0)).astype(F32)


def same_group(row, lane):
    inside = jnp.zeros(row.shape, jnp.bool_)
    for start, stop, unused_half, unused_offset in GROUPS:
        inside = inside | ((row >= start) & (row < stop) & (lane >= start) & (lane < stop))
    return inside


def prep_kernel(count_ref, line_ref, box_ref, table_ref, oh_ref, oht_ref, tab_ref):
    visual = stream_is_visual()
    tokens = line_ref.shape[1]
    heads_local, table_width = table_ref.shape
    line = jnp.where(visual, line_ref[1:2, :], line_ref[0:1, :])
    across = jnp.where(visual, box_ref[1, 0:1, :], box_ref[0, 0:1, :]) + LINES
    down = jnp.where(visual, box_ref[1, 1:2, :], box_ref[0, 1:2, :]) + (LINES + BOXES)
    level = iota((LEVELS, tokens), 0)
    wanted = jnp.where(level < LINES, line, jnp.where(level < LINES + BOXES, across, down))
    one_hot = (wanted == level).astype(F32)
    back = LEVELS - 1 - level
    wanted_back = jnp.where(back < LINES, line, jnp.where(back < LINES + BOXES, across, down))
    oht_ref[...] = (wanted_back == back).astype(F32).astype(BF16)
    closed = jnp.logical_and(visual, iota((LEVELS, tokens), 1) >= count_ref[0])
    mask = jnp.where(closed, FLOOR_SCORE, 0.0)
    oh_ref[...] = jnp.transpose(jnp.where(level == MASK_LANE, mask, one_hot)).astype(BF16)
    row = iota((LEVELS, LEVELS), 0)
    lane = iota((LEVELS, LEVELS), 1)
    inside = same_group(row, lane)
    table = table_ref[...]
    high = table.astype(BF16)
    low = (table - high.astype(F32)).astype(BF16)
    maps = [
        bucket_map(half, offset, table_width).astype(BF16)
        for unused_start, unused_stop, half, offset in GROUPS
    ]
    for part, values in enumerate((high, low)):
        spread = [dot(values, one_map) for one_map in maps]
        for head in range(heads_local):
            rows = [jnp.broadcast_to(s[head : head + 1, :], (LEVELS, LEVELS)) for s in spread]
            picked = jnp.where(
                row < LINES, rows[0], jnp.where(row < LINES + BOXES, rows[1], rows[2])
            )
            turned = pltpu.roll(picked, LEVELS // 2, 1, stride=1, stride_axis=0)
            pairs = jnp.where(inside, turned, 0.0)
            if part == 0:
                pairs = jnp.where((lane == MASK_LANE) & (row < LINES), 1.0, pairs)
            tab_ref[head, :, part * LEVELS : (part + 1) * LEVELS] = pairs.astype(BF16)


def prep(visual_count, line_index, box_index, bias_table):
    tokens = line_index.shape[1]
    heads_local = bias_table.shape[0]
    return pl.pallas_call(
        prep_kernel,
        out_shape=(
            jax.ShapeDtypeStruct((tokens, LEVELS), BF16),
            jax.ShapeDtypeStruct((LEVELS, tokens), BF16),
            jax.ShapeDtypeStruct((heads_local, LEVELS, 2 * LEVELS), BF16),
        ),
        in_specs=[pl.BlockSpec(memory_space=pltpu.SMEM)] + vmem(3),
        out_specs=tuple(vmem(3)),
        compiler_params=params(),
        name="prep",
    )(visual_count, line_index, box_index, bias_table)


def attend_kernel(
    count_ref,
    text_ref,
    visual_ref,
    stats_ref,
    w_ref,
    tab_ref,
    oh_ref,
    x_ref,
    qkv_ref,
    heads_ref,
    prob_ref,
    prob_keep,
    sems,
):
    visual = stream_is_visual()
    tokens, width = text_ref.shape
    local_width = w_ref.shape[1] // 3
    heads_local = local_width // HD
    count = count_ref[0]
    block = tokens // 2

    @pl.when(visual)
    def _():
        mean, scale, gain, shift = (stats_ref[i : i + 1, :] for i in range(4))
        for part in range(2):
            rows = pl.ds(part * block, block)
            keep = (iota((block, 1), 0) + part * block < count).astype(F32)
            centred = (visual_ref[rows, :].astype(F32) - mean) * keep
            x_ref[rows, :] = ((centred * scale * gain + shift) * keep).astype(BF16)

    @pl.when(jnp.logical_not(visual))
    def _():
        x_ref[...] = text_ref[...]

    for m in range(3):
        cols = pl.ds(m * local_width, local_width)
        qkv_ref[:, cols] = dot(x_ref[...], w_ref[:, cols]).astype(BF16)

    allowed = jnp.logical_or(jnp.logical_not(visual), iota((tokens, 1), 0) < count).astype(F32)
    one_hot = oh_ref[...]
    copies = []
    outs = []
    for head in range(heads_local):
        cols = [pl.ds(m * local_width + head * HD, HD) for m in range(3)]
        keys = jnp.concatenate([one_hot, one_hot, qkv_ref[:, cols[1]]], axis=1)
        left = dot(one_hot, tab_ref[head]).astype(BF16)
        values = qkv_ref[:, cols[2]]
        query = qkv_ref[:, cols[0]] * jnp.asarray(SCALE, BF16)
        parts = []
        for part in range(2):
            span = slice(part * block, (part + 1) * block)
            scores = dot(jnp.concatenate([left[span], query[span]], axis=1), keys, NT)
            top = jnp.max(scores, axis=1, keepdims=True)
            shifted = jnp.exp(scores - top)
            total = jnp.sum(shifted, axis=1, keepdims=True)
            prob = (shifted * (1.0 / total)).astype(BF16)
            prob_keep[head, span, :] = prob
            parts.append(dot(prob, values))
        copy = pltpu.make_async_copy(prob_keep.at[head], prob_ref.at[head], sems.at[head])
        copy.start()
        copies.append(copy)
        outs.append((jnp.concatenate(parts, axis=0) * allowed).astype(BF16))
        if head % 2 == 1:
            heads_ref[:, (head - 1) * HD : (head + 1) * HD] = jnp.concatenate(outs[-2:], axis=1)
    if heads_local % 2:
        heads_ref[:, (heads_local - 1) * HD :] = outs[-1]
    for copy in copies:
        copy.wait()


def attend(visual_count, text_in, visual_in, stats, weight, tab, one_hot):
    tokens, width = text_in.shape
    local_width = weight.shape[1] // 3
    heads_local = local_width // HD
    return pl.pallas_call(
        attend_kernel,
        out_shape=(
            jax.ShapeDtypeStruct((tokens, width), BF16),
            jax.ShapeDtypeStruct((tokens, 3 * local_width), BF16),
            jax.ShapeDtypeStruct((tokens, local_width), BF16),
            jax.ShapeDtypeStruct((heads_local, tokens, tokens), BF16),
        ),
        in_specs=[pl.BlockSpec(memory_space=pltpu.SMEM)] + vmem(6),
        out_specs=tuple(vmem(3)) + (pl.BlockSpec(memory_space=pl.ANY),),
        scratch_shapes=[
            pltpu.VMEM((heads_local, tokens, tokens), BF16),
            pltpu.SemaphoreType.DMA((heads_local,)),
        ],
        compiler_params=params(),
        name="attend",
    )(visual_count, text_in, visual_in, stats, weight, tab, one_hot)


ERF_P = 0.3275911 * 0.7071067811865476
ERF_A = (0.254829592, -0.284496736, 1.421413741, -1.453152027, 1.061405429)
VEC_ROWS = 16


def gelu_parts(pre):
    t = 1.0 / (1.0 + ERF_P * jnp.abs(pre))
    bell = jnp.exp(-0.5 * pre * pre)
    poly = 0.5 * ERF_A[4]
    for coefficient in ERF_A[3::-1]:
        poly = poly * t + 0.5 * coefficient
    tail = poly * t * bell
    cdf = jnp.where(pre >= 0.0, 1.0 - tail, tail)
    return pre * cdf, cdf + pre * (bell * 0.3989422804014327)


def normed_rows(hidden):
    average = jnp.mean(hidden, axis=-1, keepdims=True)
    centred = hidden - average
    scale = lax.rsqrt(jnp.mean(centred * centred, axis=-1, keepdims=True) + EPSILON)
    return centred * scale, scale


def normed_back(upstream, hat, scale, gain):
    scaled = upstream * gain
    return scale * (
        scaled
        - jnp.mean(scaled, axis=-1, keepdims=True)
        - hat * jnp.mean(scaled * hat, axis=-1, keepdims=True)
    )


def owner_of(half, step):
    place = lax.axis_index("dp")
    core = place & 1
    chip = place >> 1
    return ((chip ^ step) << 1) | (core if half == 0 else 1 - core)


def ffn_kernel(pieces, fused, *refs):
    (text_ref, cot_ref), refs = refs[:2], refs[2:]
    piece_refs, refs = refs[:pieces], refs[pieces:]
    (wo_hbm, w1_hbm, w2_hbm, small_ref, b1_ref), refs = refs[:5], refs[5:]
    (out_ref, share_ref, dheads_ref, dheadst_ref), refs = refs[:4], refs[4:]
    if fused:
        (mine_ref, sib_ref), refs = refs[:2], refs[2:]
        wo, w1, w2, sems, slope, act_ref, dpre_ref, low_ref, branch_ref, mix_ref, sib, vec = refs
    else:
        (act_ref, dpre_ref, low_ref, branch_ref, mix_ref, vec), refs = refs[:6], refs[6:]
        wo, w1, w2, sems, slope = refs
    copies = [
        pltpu.make_async_copy(src, dst, sems.at[i])
        for i, (src, dst) in enumerate(((wo_hbm, wo), (w1_hbm, w1), (w2_hbm, w2)))
    ]
    for copy in copies:
        copy.start()
    tokens, width = text_ref.shape
    hidden_width = w1.shape[1]
    local_width = piece_refs[0].shape[1]
    head_rank = lax.axis_index("head")
    out_bias, gain1, shift1, b2, gain2, shift2 = (small_ref[i : i + 1, :] for i in range(6))
    block = tokens // 2
    chunk = width
    chunks = hidden_width // chunk
    share = share_ref.shape[0]
    vec[...] = jnp.zeros_like(vec)
    own_rows = pl.ds(pl.multiple_of(head_rank * local_width, 64), local_width)

    def step(index, carry):
        rows = pl.ds(pl.multiple_of(index * block, block), block)

        @pl.when(index == 0)
        def _():
            copies[0].wait()

        mixed = text_ref[rows, :].astype(F32) + out_bias
        for step_index, piece in enumerate(piece_refs):
            source = head_rank ^ step_index
            wo_rows = pl.ds(pl.multiple_of(source * local_width, 64), local_width)
            mixed = mixed + dot(piece[rows, :], wo[wo_rows, :])
        hat1, scale1 = normed_rows(mixed)
        after = hat1 * gain1 + shift1
        after_low = after.astype(BF16)
        low_ref[rows, :] = after_low

        @pl.when(index == 0)
        def _():
            copies[1].wait()
            copies[2].wait()

        branch = jnp.zeros((block, width), F32)
        for c in range(chunks):
            cols = pl.ds(c * chunk, chunk)
            pre = dot(after_low, w1[:, cols]) + b1_ref[c : c + 1, :]
            act, derivative = gelu_parts(pre)
            slope[:, cols] = derivative
            act = act.astype(BF16)
            act_ref[rows, cols] = act
            branch = branch + dot(act, w2[cols, :])
        hat2, scale2 = normed_rows(after + (branch + b2))
        out_ref[rows, :] = (hat2 * gain2 + shift2).astype(BF16)
        upstream = cot_ref[rows, :].astype(F32)
        dh_two = normed_back(upstream, hat2, scale2, gain2)
        dbranch = dh_two.astype(BF16)
        branch_ref[rows, :] = dbranch
        vec[7:8, :] += jnp.sum(dbranch.astype(F32), axis=0, keepdims=True)
        vec[8:9, :] += jnp.sum(upstream * hat2, axis=0, keepdims=True)
        vec[9:10, :] += jnp.sum(upstream, axis=0, keepdims=True)
        dy = dh_two
        for c in range(chunks):
            cols = pl.ds(c * chunk, chunk)
            dpre = (dot(dbranch, w2[cols, :], NT) * slope[:, cols]).astype(BF16)
            dpre_ref[rows, cols] = dpre
            vec[3 + c : 4 + c, :] += jnp.sum(dpre.astype(F32), axis=0, keepdims=True)
            dy = dy + dot(dpre, w1[:, cols], NT)
        dh_one = normed_back(dy, hat1, scale1, gain1)
        vec[0:1, :] += jnp.sum(dh_one, axis=0, keepdims=True)
        vec[1:2, :] += jnp.sum(dy * hat1, axis=0, keepdims=True)
        vec[2:3, :] += jnp.sum(dy, axis=0, keepdims=True)
        per_block = block // share
        for part in range(per_block):

            @pl.when(index * per_block + part == head_rank)
            def _():
                share_ref[...] = dh_one[part * share : (part + 1) * share]

        dmix = dh_one.astype(BF16)
        mix_ref[rows, :] = dmix
        dheads_ref[rows, :] = dot(dmix, wo[own_rows, :], NT).astype(BF16)
        dheadst_ref[:, rows] = dot(wo[own_rows, :], dmix, NT).astype(BF16)
        return carry

    lax.fori_loop(0, tokens // block, step, 0)
    if not fused:
        return

    owners = [owner_of(half, k) for half in range(2) for k in range(4)]
    width_own = width // 8
    part_in = width_own // 4
    window = hidden_width // 8
    part_out = window // 4
    targets = [mine_ref.at[k] for k in range(4)] + [sib.at[k] for k in range(4)]
    lane = iota((part_in, width), 1)
    row = iota((part_in, width), 0)
    pick = jnp.concatenate(
        [
            (lane == owner * width_own + head_rank * part_in + row).astype(F32)
            for owner in owners
        ],
        axis=0,
    ).astype(BF16)
    low_t = dot(pick, low_ref[...], NT).astype(BF16)
    for c in range(chunks):
        grad = dot(low_t, dpre_ref[:, c * chunk : (c + 1) * chunk])
        for n, target in enumerate(targets):
            target[c * part_in : (c + 1) * part_in, :] = grad[n * part_in : (n + 1) * part_in]
    base = chunks * part_in
    pick = (
        iota((part_out, window), 1) == head_rank * part_out + iota((part_out, window), 0)
    ).astype(F32).astype(BF16)
    for owner, target in zip(owners, targets):
        cols = pl.ds(pl.multiple_of(owner * window, 128), window)
        act_t = dot(pick, act_ref[:, cols], NT).astype(BF16)
        target[base : base + part_out, :] = dot(act_t, branch_ref[...])
    base += part_out
    lane = iota((width_own, width), 1)
    row = iota((width_own, width), 0)
    half_own = width_own // 2
    for owner, target in zip(owners, targets):
        pick = (lane == owner * width_own + row).astype(F32).astype(BF16)
        mix_t = dot(pick, mix_ref[...], NT).astype(BF16)
        grad = dot(mix_t, piece_refs[0][...])
        target[base : base + half_own, :] = jnp.concatenate(
            [grad[:half_own], grad[half_own:]], axis=1
        )
    base += half_own
    for target in targets:
        target[base : base + VEC_ROWS, :] = vec[...]
    for k in range(4):
        sib_ref[k] = sib[k].astype(BF16)


def ffn(text_in, cotangent, pieces, out_weight, w1, w2, small, b1, share, fused):
    tokens, width = text_in.shape
    hidden_width = w1.shape[1]
    local_width = pieces[0].shape[1]
    block = tokens // 2
    weights = [
        pltpu.VMEM(out_weight.shape, BF16),
        pltpu.VMEM(w1.shape, BF16),
        pltpu.VMEM(w2.shape, BF16),
        pltpu.SemaphoreType.DMA((3,)),
        pltpu.VMEM((block, hidden_width), F32),
    ]
    kept = [
        ((tokens, hidden_width), BF16),
        ((tokens, hidden_width), BF16),
        ((tokens, width), BF16),
        ((tokens, width), BF16),
        ((tokens, width), BF16),
    ]
    outs = [
        jax.ShapeDtypeStruct((tokens, width), BF16),
        jax.ShapeDtypeStruct((share, width), F32),
        jax.ShapeDtypeStruct((tokens, local_width), BF16),
        jax.ShapeDtypeStruct((local_width, tokens), BF16),
    ]
    if fused:
        rows = 2 * (hidden_width // 32) + width // 16 + VEC_ROWS
        outs += [
            jax.ShapeDtypeStruct((4, rows, width), F32),
            jax.ShapeDtypeStruct((4, rows, width), BF16),
        ]
        scratch = weights + [pltpu.VMEM(*entry) for entry in kept]
        scratch += [pltpu.VMEM((4, rows, width), F32), pltpu.VMEM((VEC_ROWS, width), F32)]
    else:
        outs += [jax.ShapeDtypeStruct(*entry) for entry in kept]
        outs += [jax.ShapeDtypeStruct((VEC_ROWS, width), F32)]
        scratch = weights
    return pl.pallas_call(
        functools.partial(ffn_kernel, len(pieces), fused),
        out_shape=tuple(outs),
        in_specs=vmem(2 + len(pieces)) + [pl.BlockSpec(memory_space=pl.ANY)] * 3 + vmem(2),
        out_specs=tuple(vmem(len(outs))),
        scratch_shapes=scratch,
        compiler_params=params(),
        name="ffn",
    )(text_in, cotangent, *pieces, out_weight, w1, w2, small, b1)


def attend_back_kernel(
    count_ref,
    qkv_ref,
    heads_ref,
    dheads_ref,
    dheadst_ref,
    oh_ref,
    oht_ref,
    w_ref,
    visual_ref,
    stats_ref,
    prob_hbm,
    *refs,
):
    steps = lax.axis_size("head")
    dqkv_ref, pair_ref, sums_ref = refs[:3]
    part_refs = refs[3 : 3 + steps]
    prob_keep, sems = refs[3 + steps :]
    visual = stream_is_visual()
    tokens = qkv_ref.shape[0]
    local_width = qkv_ref.shape[1] // 3
    heads_local = local_width // HD
    count = count_ref[0]
    copies = [
        pltpu.make_async_copy(prob_hbm.at[head], prob_keep.at[head], sems.at[head])
        for head in range(heads_local)
    ]
    for copy in copies:
        copy.start()
    open_row = jnp.logical_or(jnp.logical_not(visual), iota((tokens, 1), 0) < count)
    open_lane = jnp.logical_or(jnp.logical_not(visual), iota((1, tokens), 1) < count)
    allowed = open_row.astype(BF16)
    allowed_lane = open_lane.astype(BF16)
    one_hot = oh_ref[...]
    one_hot_t = oht_ref[...]
    inside = same_group(LEVELS - 1 - iota((LEVELS, LEVELS), 0), iota((LEVELS, LEVELS), 1))
    eye = (iota((HD, HD), 0) == iota((HD, HD), 1)).astype(F32).astype(BF16)
    extra = jnp.concatenate(
        [jnp.ones((tokens, 2), F32), jnp.zeros((tokens, HD - 2), F32)], axis=1
    ).astype(BF16)
    lane = iota((tokens, HD), 1)
    turned = [[], [], []]
    for head in range(heads_local):
        cols = [pl.ds(m * local_width + head * HD, HD) for m in range(3)]
        own = slice(head * HD, (head + 1) * HD)
        query, keys, values = (qkv_ref[:, c] for c in cols)
        dout = dheads_ref[:, own] * allowed
        dout_t = dheadst_ref[own, :] * allowed_lane
        inner = -jnp.sum(
            dout.astype(F32) * heads_ref[:, own].astype(F32), axis=1, keepdims=True
        )
        high = inner.astype(BF16).astype(F32)
        tail = jnp.where(lane == 0, high, jnp.where(lane == 1, inner - high, 0.0)).astype(BF16)
        copies[head].wait()
        centred = dot(
            jnp.concatenate([dout, tail], axis=1), jnp.concatenate([values, extra], axis=1), NT
        )
        prob = prob_keep[head]
        dscore = (prob.astype(F32) * centred).astype(BF16)
        both = dot(dscore, jnp.concatenate([one_hot, keys], axis=1))
        level_high = both[:, :LEVELS].astype(BF16)
        level_low = (both[:, :LEVELS] - level_high.astype(F32)).astype(BF16)
        pairs = dot(one_hot_t, level_high) + dot(one_hot_t, level_low)
        pair_ref[head] = jnp.where(inside, pairs, 0.0)
        turned[0].append(both[:, LEVELS:] * SCALE)
        query_t = dot(eye, query, NT).astype(BF16)
        turned[1].append(dot(query_t, dscore) * SCALE)
        turned[2].append(dot(dout_t, prob))
        if head % 2 == 1 or head == heads_local - 1:
            start = head - head % 2
            span = HD * len(turned[0])
            for m in range(3):
                joined = jnp.concatenate(turned[m], axis=1 if m == 0 else 0)
                if m:
                    joined = jnp.transpose(joined)
                dqkv_ref[:, pl.ds(m * local_width + start * HD, span)] = joined.astype(BF16)
            turned = [[], [], []]

    head_rank = lax.axis_index("head")
    share = tokens // steps
    mean, scale = stats_ref[0:1, :], stats_ref[1:2, :]
    shift_sum = jnp.zeros(mean.shape, F32)
    gain_sum = jnp.zeros(mean.shape, F32)
    for k in range(steps):
        start = pl.multiple_of((head_rank ^ k) * share, share)
        rows = pl.ds(start, share)
        part = dot(dqkv_ref[rows, :], w_ref[...], NT)
        part_refs[k][...] = part.astype(BF16)
        keep = jnp.logical_and(visual, iota((share, 1), 0) + start < count).astype(F32)
        kept = part * keep
        shift_sum = shift_sum + jnp.sum(kept, axis=0, keepdims=True)
        hat = (visual_ref[rows, :].astype(F32) - mean) * scale
        gain_sum = gain_sum + jnp.sum(kept * hat, axis=0, keepdims=True)
    sums_ref[...] = jnp.concatenate(
        [shift_sum, gain_sum, jnp.zeros((6, mean.shape[1]), F32)], axis=0
    )


def attend_back(
    visual_count, qkv, heads, dheads, dheads_t, one_hot, one_hot_t, weight, visual_in, stats, prob
):
    tokens, width = visual_in.shape
    local_width = heads.shape[1]
    heads_local = local_width // HD
    steps = lax.axis_size("head")
    return pl.pallas_call(
        attend_back_kernel,
        out_shape=(
            jax.ShapeDtypeStruct((tokens, 3 * local_width), BF16),
            jax.ShapeDtypeStruct((heads_local, LEVELS, LEVELS), F32),
            jax.ShapeDtypeStruct((8, width), F32),
        )
        + tuple(jax.ShapeDtypeStruct((tokens // steps, width), BF16) for k in range(steps)),
        in_specs=[pl.BlockSpec(memory_space=pltpu.SMEM)]
        + vmem(9)
        + [pl.BlockSpec(memory_space=pl.ANY)],
        out_specs=tuple(vmem(3 + steps)),
        scratch_shapes=[
            pltpu.VMEM((heads_local, tokens, tokens), BF16),
            pltpu.SemaphoreType.DMA((heads_local,)),
        ],
        compiler_params=params(),
        name="attend_back",
    )(
        visual_count,
        qkv,
        heads,
        dheads,
        dheads_t,
        one_hot,
        one_hot_t,
        weight,
        visual_in,
        stats,
        prob,
    )


def qkv_grad_kernel(fused, x_ref, dqkv_ref, pair_ref, *refs):
    tokens, width = x_ref.shape
    heads_local = pair_ref.shape[0]
    table_width = NB_REL + 2 * NB_BOX
    sums = [[], [], []]
    for head in range(heads_local):
        back = pltpu.roll(pair_ref[head], LEVELS // 2 + 1, 1, stride=1, stride_axis=0)
        for n, (start, stop, unused_half, unused_offset) in enumerate(GROUPS):
            rows = back[LEVELS - stop : LEVELS - start]
            sums[n].append(jnp.sum(rows, axis=0, keepdims=True))
    table = jnp.zeros((8, table_width), F32)
    for n, (unused_start, unused_stop, half, offset) in enumerate(GROUPS):
        stacked = jnp.concatenate(
            sums[n] + [jnp.zeros((8 - heads_local, LEVELS), F32)], axis=0
        )
        spread = bucket_map(half, offset, table_width).astype(BF16)
        high = stacked.astype(BF16)
        rest = stacked - high.astype(F32)
        low = rest.astype(BF16)
        lowest = (rest - low.astype(F32)).astype(BF16)
        for piece in (high, low, lowest):
            table = table + dot(piece, spread, NT)
    if not fused:
        grad_ref, table_ref = refs
        table_ref[...] = table
        eye = (iota((width, width), 0) == iota((width, width), 1)).astype(F32).astype(BF16)
        x_t = dot(eye, x_ref[...], NT).astype(BF16)
        grad_ref[...] = dot(x_t, dqkv_ref[...]).astype(BF16)
        return
    mine_ref, sib_ref = refs
    width_own = width // 8
    lane = iota((width_own, width), 1)
    row = iota((width_own, width), 0)
    columns = dqkv_ref.shape[1]
    padded = jnp.concatenate(
        [
            jnp.concatenate([table, jnp.zeros((8, columns - table_width), F32)], axis=1),
            jnp.zeros((8, columns), F32),
        ],
        axis=0,
    )
    for half, target in ((1, sib_ref), (0, mine_ref)):
        pick = jnp.concatenate(
            [(lane == owner_of(half, k) * width_own + row).astype(F32) for k in range(4)], axis=0
        ).astype(BF16)
        x_t = dot(pick, x_ref[...], NT).astype(BF16)
        grad = dot(x_t, dqkv_ref[...])
        for k in range(4):
            target[k] = jnp.concatenate(
                [grad[k * width_own : (k + 1) * width_own], padded], axis=0
            ).astype(target.dtype)


def qkv_grad(x, dqkv, pairs, fused):
    tokens, width = x.shape
    columns = dqkv.shape[1]
    if fused:
        rows = width // 8 + 16
        outs = (
            jax.ShapeDtypeStruct((4, rows, columns), F32),
            jax.ShapeDtypeStruct((4, rows, columns), BF16),
        )
    else:
        outs = (
            jax.ShapeDtypeStruct((width, columns), BF16),
            jax.ShapeDtypeStruct((8, NB_REL + 2 * NB_BOX), F32),
        )
    return pl.pallas_call(
        functools.partial(qkv_grad_kernel, fused),
        out_shape=outs,
        in_specs=vmem(3),
        out_specs=tuple(vmem(2)),
        compiler_params=params(),
        name="qkv_grad",
    )(x, dqkv, pairs)


def swap(value, axis, mask):
    size = lax.axis_size(axis)
    return lax.ppermute(value, axis, [(i, i ^ mask) for i in range(size)])


def owned_sum(mine, sib):
    joined = mine + swap(sib, "dp", 1).astype(F32)
    total = joined[0]
    for k in range(1, 4):
        total = total + swap(joined[k].astype(BF16), "dp", k << 1).astype(F32)
    return total


def small_sum(value, fused):
    if not fused:
        return lax.psum(value, ("dp", "head"))
    value = value + swap(value, "dp", 1)
    value = value + swap(value, "dp", 2) + swap(value, "dp", 4) + swap(value, "dp", 6)
    return value + swap(value, "head", 1) + swap(value, "head", 2) + swap(value, "head", 3)


def batch_stats(visual, valid_rows, fused):
    count = jnp.sum(valid_rows)
    sums = jnp.sum(visual * valid_rows, axis=0)
    centred = (visual - sums / count) * valid_rows
    squares = jnp.sum(centred * centred, axis=0)
    packed = jnp.stack([sums, squares, jnp.full_like(sums, count)])

    def join(blocks):
        total = functools.reduce(jnp.add, (b[0] for b in blocks))
        number = functools.reduce(jnp.add, (b[2] for b in blocks))
        mean = total / number
        spread = functools.reduce(
            jnp.add, (b[1] + b[2] * (b[0] / b[2] - mean) ** 2 for b in blocks)
        )
        return jnp.stack([total, spread, number])

    if fused:
        packed = join([packed, swap(packed, "dp", 1)])
        packed = join([packed] + [swap(packed, "dp", k) for k in (2, 4, 6)])
    else:
        gathered = lax.all_gather(packed, "dp")
        packed = join([gathered[i] for i in range(gathered.shape[0])])
    total, spread, number = packed
    return total / number, lax.rsqrt(spread / number + EPSILON), number[0]


def per_device(
    text_in,
    visual_in,
    visual_count,
    line_index,
    box_index,
    qkv_weight,
    bias_table,
    out_weight,
    out_bias,
    norm1_gain,
    norm1_shift,
    ffn_weight_in,
    ffn_bias_in,
    ffn_weight_out,
    ffn_bias_out,
    norm2_gain,
    norm2_shift,
    batch_gain,
    batch_shift,
    cotangent,
):
    tokens, width = text_in.shape
    local_width = qkv_weight.shape[2]
    heads_local = local_width // HD
    head_count = lax.axis_size("head")
    dp_count = lax.axis_size("dp")
    head_rank = lax.axis_index("head")
    dp_rank = lax.axis_index("dp")
    fused = head_count == 4 and dp_count == 8
    share = tokens // head_count
    first_row = head_rank * share
    hidden_width = ffn_weight_in.shape[1]
    table_width = bias_table.shape[1]

    valid_rows = (jnp.arange(tokens, dtype=jnp.int32) < visual_count[0]).astype(F32)[:, None]
    mean, batch_scale, total_count = batch_stats(visual_in.astype(F32), valid_rows, fused)
    stats = jnp.concatenate(
        [jnp.stack([mean, batch_scale, batch_gain, batch_shift]), jnp.zeros((4, width), F32)]
    )
    weight = qkv_weight.reshape(width, 3 * local_width)
    one_hot, one_hot_t, tab = prep(visual_count, line_index, box_index, bias_table)
    x, qkv, heads, prob = attend(visual_count, text_in, visual_in, stats, weight, tab, one_hot)
    pieces = [heads] + [swap(heads, "head", k) for k in range(1, head_count)]
    small = jnp.concatenate(
        [
            jnp.stack(
                [out_bias, norm1_gain, norm1_shift, ffn_bias_out, norm2_gain, norm2_shift]
            ),
            jnp.zeros((2, width), F32),
        ]
    )
    results = ffn(
        text_in,
        cotangent,
        pieces,
        out_weight,
        ffn_weight_in,
        ffn_weight_out,
        small,
        ffn_bias_in.reshape(hidden_width // width, width),
        share,
        fused,
    )
    layer_out, dh_share, dheads, dheads_t = results[:4]
    part_in = width // (dp_count * head_count)
    part_out = hidden_width // (dp_count * head_count)
    own_in = dp_rank * (width // dp_count) + head_rank * part_in
    if fused:
        mine, sib = results[4:]
        total = owned_sum(mine, sib)
        chunks = hidden_width // width
        base = chunks * part_in
        grad_ffn_in = jnp.transpose(
            total[:base].reshape(chunks, part_in, width), (1, 0, 2)
        ).reshape(part_in, hidden_width)
        grad_ffn_out = total[base : base + part_out]
        base += part_out
        half_own = width // dp_count // 2
        packed = total[base : base + half_own]
        grad_out_weight = jnp.transpose(
            jnp.concatenate([packed[:, :local_width], packed[:, local_width:]], axis=0)
        )
        vec = total[base + half_own :]
    else:
        act, dpre, after_low, dbranch, dmix, vec = results[4:]

        def scatter(value, dimension):
            return lax.psum_scatter(
                value.astype(BF16), "dp", scatter_dimension=dimension, tiled=True
            ).astype(F32)

        def own_columns(value, part):
            split = value.reshape(tokens, dp_count, head_count, part)
            return lax.dynamic_index_in_dim(split, head_rank, 2, keepdims=False).reshape(
                tokens, dp_count * part
            )

        grad_ffn_in = scatter(dot(own_columns(after_low, part_in), dpre, TN), 0)
        grad_ffn_out = scatter(dot(own_columns(act, part_out), dbranch, TN), 0)
        grad_out_weight = scatter(dot(heads, dmix, TN), 1)
        vec = lax.psum(vec.astype(BF16), "dp").astype(F32)

    def own_slice(index):
        return lax.dynamic_slice_in_dim(vec[index], own_in, part_in, 0)

    grad_ffn_bias_in = lax.dynamic_slice_in_dim(
        vec[3 : 3 + hidden_width // width].reshape(hidden_width),
        dp_rank * (hidden_width // dp_count) + head_rank * part_out,
        part_out,
        0,
    )

    dqkv, pairs, sums, *parts = attend_back(
        visual_count,
        qkv,
        heads,
        dheads,
        dheads_t,
        one_hot,
        one_hot_t,
        weight,
        visual_in,
        stats,
        prob,
    )
    received = [parts[0].astype(F32)] + [
        swap(parts[k], "head", k).astype(F32) for k in range(1, head_count)
    ]
    sums = small_sum(sums[:2], fused)
    if fused:
        grads = owned_sum(*qkv_grad(x, dqkv, pairs, True))
        own = width // dp_count
        grad_qkv = grads[:own].reshape(own, 3, local_width)
        table = grads[own : own + heads_local, :table_width]
        own = table_width // dp_count
        grad_bias_table = lax.dynamic_slice_in_dim(table, dp_rank * own, own, 1)
    else:
        grad, table = qkv_grad(x, dqkv, pairs, False)
        grad_qkv = scatter(grad.reshape(width, 3, local_width), 0)
        grad_bias_table = scatter(table[:heads_local], 1)

    half = head_count // 2
    same = functools.reduce(jnp.add, received[:half])
    other = functools.reduce(jnp.add, received[half:])
    visual = head_rank >= half
    grad_text = dh_share + jnp.where(visual, other, same)
    valid_share = lax.dynamic_slice_in_dim(valid_rows, first_row, share, 0)
    hat = (
        (lax.dynamic_slice_in_dim(visual_in, first_row, share, 0).astype(F32) - mean)
        * valid_share
        * batch_scale
    )
    dnormed = jnp.where(visual, same, other) * valid_share
    shift_gradient, gain_gradient = sums[0], sums[1]
    grad_visual = (
        valid_share
        * batch_scale
        * batch_gain
        * (dnormed - shift_gradient / total_count - hat * gain_gradient / total_count)
    )
    return (
        layer_out,
        grad_text,
        grad_visual,
        grad_qkv,
        grad_bias_table,
        grad_out_weight,
        own_slice(0),
        own_slice(1),
        own_slice(2),
        grad_ffn_in,
        grad_ffn_bias_in,
        grad_ffn_out,
        own_slice(7),
        own_slice(8),
        own_slice(9),
        gain_gradient,
        shift_gradient,
    )


def solution(mesh):
    in_specs = (
        P("dp", None),
        P("dp", None),
        P("dp"),
        P(None, "dp"),
        P(None, None, "dp"),
        P(None, None, "head"),
        P("head", None),
        P(),
        P(),
        P(),
        P(),
        P(),
        P(),
        P(),
        P(),
        P(),
        P(),
        P(),
        P(),
        P("dp", None),
    )
    out_specs = (
        P("dp", None),
        P(("dp", "head"), None),
        P(("dp", "head"), None),
        P("dp", None, "head"),
        P("head", "dp"),
        P("head", "dp"),
        P(("dp", "head")),
        P(("dp", "head")),
        P(("dp", "head")),
        P(("dp", "head"), None),
        P(("dp", "head")),
        P(("dp", "head"), None),
        P(("dp", "head")),
        P(("dp", "head")),
        P(("dp", "head")),
        P(),
        P(),
    )
    return jax.shard_map(
        per_device, mesh=mesh, in_specs=in_specs, out_specs=out_specs, check_vma=False
    )
```

time: 423 us -> 197 us (0.47)
  matrix products: 115 us -> 0 us
  blocking collectives: 92.1 us -> 0 us
  waiting for transfers between devices: 145 us -> 67 us
  Pallas kernels: 0 us -> 67.5 us
  starting transfers between devices: 0.67 us -> 30.2 us
  other arithmetic: 30.6 us -> 11.4 us
  between operations: 18.3 us -> 1.7 us
    dot_general x36 -> x0, matrix products: 115 us -> none  [the longest x1 19.6 us: per_device(): jnp.dot(after_low, ffn_weight_in, preferred_element_type=jnp.float32)]
    reduce_scatter x5 -> x0, waiting for transfers between devices: 109 us -> none  [the longest x2 67.5 us: per_device(): lax.psum_scatter(as_sent((jnp.sum(dh_one, axis=0), jnp.sum(dy_one * hat_o...]
    psum x3 -> x0, blocking collectives: 67.9 us -> none  [the longest x1 39.5 us: per_device(): lax.psum((jnp.sum(normed_gradient, axis=0), jnp.sum(normed_gradient * nor...]
    pallas_call x0 -> x5, Pallas kernels: none -> 67.5 us  [the longest x1 33.9 us: ffn(): pl.pallas_call(functools.partial(ffn_kernel, len(pieces), fused), out_sha...]
    ppermute x0 -> x25, waiting for transfers between devices: none -> 67 us  [swap(): return lax.ppermute(value, axis, [(i, i ^ mask) for i in range(size)])]
    all_gather x1 -> x0, waiting for transfers between devices: 35.4 us -> none  [per_device(): lax.all_gather(heads_out, 'head', axis=1, tiled=True)]
    ppermute x0 -> x25, starting transfers between devices: none -> 30.2 us  [swap(): return lax.ppermute(value, axis, [(i, i ^ mask) for i in range(size)])]
    unnamed x1 -> x0, blocking collectives: 24.2 us -> none
  transfers between devices with their start and end apart: 6 -> 25, of which waited for: 5 -> 15; matrix products, arithmetic and copies ran while one was open for 12% -> 8% of each run, Pallas kernels for 0% -> 4%
where the time goes in v1:
time: 197 us; the launch traced here: 195 us
  Pallas kernels  67.5 us (34%)
  waiting for transfers between devices  67 us (34%)
  starting transfers between devices  30.2 us (15%)
  local copies, waits for them, and re-layouts  17.3 us (9%)
  other arithmetic  11.4 us (6%)
    ppermute x25, waiting for transfers between devices, swap(): return lax.ppermute(value, axis, [(i, i ^ mask) for i in range(size)])  67 us
    pallas_call x1, Pallas kernels, ffn(): pl.pallas_call(functools.partial(ffn_kernel, len(pieces), fused), out_sha...  33.9 us
    ppermute x25, starting transfers between devices, swap(): return lax.ppermute(value, axis, [(i, i ^ mask) for i in range(size)])  30.2 us
    pallas_call x1, Pallas kernels, attend_back(): pl.pallas_call(attend_back_kernel, out_shape=(jax.ShapeDtypeStruct((token...  13.8 us
    pallas_call x1, Pallas kernels, attend(): pl.pallas_call(attend_kernel, out_shape=(jax.ShapeDtypeStruct((tokens, wi...  12.7 us
    pallas_call x1, Pallas kernels, qkv_grad(): pl.pallas_call(functools.partial(qkv_grad_kernel, fused), out_shape=outs,...  5.28 us
    unnamed x31, local copies, waits for them, and re-layouts  4.16 us
  transfers between devices with their start and end apart: 25, of which 15 were waited for; matrix products, arithmetic and copies ran while one was open for 8% of the time, Pallas kernels for 4%

profile of v1, /device:TPU:0, one launch (start us, length us, event | category | flops | bytes accessed | tf_op | source)
XLA Modules:
  0.0 195.0 jit_solution(7192707520455462430)
XLA Ops:
  1.9 1.4 fusion
  3.9 1.4 fusion.3
  6.6 0.8 collective-permute-done
  7.4 0.7 fusion.15
  8.1 3.9 %collective-permute-start.3 = (f32[3,768]{1,0:T(4,128)S(1)}, f32[3,768]{1,0:T(4,128)S(1)}, u32[]{:S(2)}, u32[]{:S(2)}) collective-permute-start(f32[3,768]{1,0:T(4,128)S(1)} %pad_maximum_fusion.1), channel_id=1, source_target_pairs={{0,24},{4,28},{8,16},{12,20},{16,8},{20,12},{24,0},{28,4},{1,25},{... | collective-permute-start | bytes 27656 | tf_op jit(solution)/shard_map/ppermute | solution.py:670
  12.6 0.7 stack.43
  13.3 0.7 stack.42
  14.0 2.6 %copy.40 = bf16[768,3,384]{0,2,1:T(8,128)(2,1)S(1)} copy(bf16[768,3,384]{2,0,1:T(8,128)(2,1)} %param.25) | data formatting | bytes 3538944 | tf_op args[5]
  16.6 2.3 %copy.41.w_ref = bf16[768,1152]{1,0:T(8,128)(2,1)} copy(bf16[768,1152]{0,1:T(8,128)(2,1)S(1)} %bitcast.56) | data formatting | bytes 3538944 | tf_op jit(solution)/shard_map/reshape | solution.py:755
  18.9 1.8 prep.1
  21.4 12.7 %attend.1 = (bf16[512,768]{1,0:T(8,128)(2,1)}, bf16[512,1152]{1,0:T(8,128)(2,1)}, bf16[512,384]{1,0:T(8,128)(2,1)}, bf16[6,512,512]{2,1,0:T(8,128)(2,1)}) custom-call(s32[1]{0:T(128)} %copy.49.count_ref, bf16[512,768]{1,0:T(8,128)(2,1)} %refs_0_.1, bf16[512,768]{1,0:T(8,128)(2,1)} %visual_ref.3, f32[8,768]{1,0:T(8,128)} %concatenate.9.stats_ref, ...), custom_call_target="tpu_custom_call" | custom-call | tf_op jit(solution)/shard_map/attend/pallas_call | solution.py:204
  34.1 4.4 %collective-permute-start.6 = (bf16[512,384]{1,0:T(8,128)(2,1)}, bf16[512,384]{1,0:T(8,128)(2,1)S(1)}, u32[]{:S(2)}, u32[]{:S(2)}) collective-permute-start(bf16[512,384]{1,0:T(8,128)(2,1)} %get-tuple-element.41.refs_2_.heads_ref), channel_id=1, source_target_pairs={{0,3},{1,2},{2,1},{3,0},{4,7},{5,6},{6,5},{7,4},{8,11},{9,10},{10,... | collective-permute-start | bytes 1179656 | tf_op jit(solution)/shard_map/ppermute | solution.py:670
  40.6 8.3 %collective-permute-done.6.refs_5_ = bf16[512,384]{1,0:T(8,128)(2,1)S(1)} collective-permute-done((bf16[512,384]{1,0:T(8,128)(2,1)}, bf16[512,384]{1,0:T(8,128)(2,1)S(1)}, u32[]{:S(2)}, u32[]{:S(2)}) %collective-permute-start.6) | collective-permute-done | bytes 393248 | tf_op jit(solution)/shard_map/ppermute | solution.py:670
  48.9 22.8 %collective-permute-done.5.refs_4_ = bf16[512,384]{1,0:T(8,128)(2,1)S(1)} collective-permute-done((bf16[512,384]{1,0:T(8,128)(2,1)}, bf16[512,384]{1,0:T(8,128)(2,1)S(1)}, u32[]{:S(2)}, u32[]{:S(2)}) %collective-permute-start.5) | collective-permute-done | bytes 393248 | tf_op jit(solution)/shard_map/ppermute | solution.py:670
  71.6 0.7 copy-done.4
  72.4 0.7 copy-done.5
  73.1 33.9 %ffn.1 = (bf16[512,768]{1,0:T(8,128)(2,1)}, f32[128,768]{1,0:T(8,128)}, bf16[512,384]{1,0:T(8,128)(2,1)}, bf16[384,512]{1,0:T(8,128)(2,1)}, f32[4,256,768]{2,1,0:T(8,128)}, /*index=5*/bf16[4,256,768]{2,1,0:T(8,128)(2,1)}) custom-call(bf16[512,768]{1,0:T(8,128)(2,1)} %refs_0_.1, bf16[512,768]{1,0:T(8,128)(2,1)} %refs_1_.1, ...), custom_call_target="tpu_custom_call" | custom-call | tf_op jit(solution)/shard_map/ffn/pallas_call | solution.py:442
  107.1 13.8 %attend_back.1 = (bf16[512,1152]{1,0:T(8,128)(2,1)}, f32[6,128,128]{2,1,0:T(8,128)}, f32[8,768]{1,0:T(8,128)}, bf16[128,768]{1,0:T(8,128)(2,1)}, bf16[128,768]{1...) custom-call(s32[1]{0:T(128)} %copy.49.count_ref, bf16[512,1152]{1,0:T(8,128)(2,1)} %get-tuple-element.44.qkv_ref, ...), custom_call_target="tpu_custom_call" | custom-call | tf_op jit(solution)/shard_map/attend_back/pallas_call | solution.py:558
  120.9 0.8 slice.153
  121.7 5.3 %qkv_grad.1 = (f32[4,112,1152]{2,1,0:T(8,128)}, bf16[4,112,1152]{2,1,0:T(8,128)(2,1)}) custom-call(bf16[512,768]{1,0:T(8,128)(2,1)} %get-tuple-element.54.x_ref, bf16[512,1152]{1,0:T(8,128)(2,1)} %get-tuple-element.55.dqkv_ref, f32[6,128,128]{2,1,0:T(8,128)} %get-tuple-element.56.pair_ref), custom_call_target="tpu_custom_call" | custom-call | tf_op jit(solution)/shard_map/qkv_grad/pallas_call | solution.py:658
  127.5 0.9 slice_add_fusion.6
  128.3 2.4 %collective-permute-start.13 = (f32[2,768]{1,0:T(2,128)S(1)}, f32[2,768]{1,0:T(2,128)S(1)}, u32[]{:S(2)}, u32[]{:S(2)}) collective-permute-start(f32[2,768]{1,0:T(2,128)S(1)} %slice_add_fusion.6), channel_id=1, source_target_pairs={{0,24},{4,28},{8,16},{12,20},{16,8},{20,12},{24,0},{28,4},{1,25},{... | collective-permute-start | bytes 18440 | tf_op jit(solution)/shard_map/ppermute | solution.py:670
  131.8 1.0 collective-permute-done.13
  132.9 1.5 collective-permute-done.12
  134.9 2.7 %collective-permute-start.16 = (f32[2,768]{1,0:T(2,128)S(1)}, f32[2,768]{1,0:T(2,128)S(1)}, u32[]{:S(2)}, u32[]{:S(2)}) collective-permute-start(f32[2,768]{1,0:T(2,128)S(1)} %add_add_fusion.1), channel_id=1, source_target_pairs={{0,3},{1,2},{2,1},{3,0},{4,7},{5,6},{6,5},{7,4},{8,11},{9,10},{10,... | collective-permute-start | bytes 18440 | tf_op jit(solution)/shard_map/ppermute | solution.py:670
  137.6 1.7 collective-permute-start.14
  140.0 1.3 collective-permute-start.7
  141.2 1.8 collective-permute-start.8
  143.1 3.9 %collective-permute-done.15 = f32[2,768]{1,0:T(2,128)S(1)} collective-permute-done((f32[2,768]{1,0:T(2,128)S(1)}, f32[2,768]{1,0:T(2,128)S(1)}, u32[]{:S(2)}, u32[]{:S(2)}) %collective-permute-start.15) | collective-permute-done | bytes 6176 | tf_op jit(solution)/shard_map/ppermute | solution.py:670
  147.0 1.3 slice_reduce_fusion.1
  148.3 5.9 %collective-permute-done.7 = bf16[128,768]{1,0:T(8,128)(2,1)S(1)} collective-permute-done((bf16[128,768]{1,0:T(8,128)(2,1)}, bf16[128,768]{1,0:T(8,128)(2,1)S(1)}, u32[]{:S(2)}, u32[]{:S(2)}) %collective-permute-start.7) | collective-permute-done | bytes 196640 | tf_op jit(solution)/shard_map/ppermute | solution.py:670
  154.2 1.9 collective-permute-done.9
  156.1 2.8 %subtract_multiply_fusion = (f32[128,768]{1,0:T(8,128)}, f32[128,768]{1,0:T(8,128)}) fusion(bf16[128,768]{1,0:T(8,128)(2,1)S(1)} %collective-permute-done.8, bf16[128,768]{1,0:T(8,128)(2,1)S(1)} %collective-permute-done.7, bf16[128,768]{1,0:T(8,128)(2,1)S(1)} %collective-permute-done.9, bf16[128,768]{1,0:T(8,128)(2,1)} %get-tuple-element.51, f32[]{:T(128)} %bitcast.2, ...), kind=kLoop, calls=%fused_computation.20 | loop fusion | flops 2064384 | bytes 2178569 | tf_op jit(solution)/shard_map/mul | solution.py:871
  159.2 0.8 collective-permute-start.18
  160.1 2.4 %collective-permute-start.20 = (bf16[112,1152]{1,0:T(8,128)(2,1)S(1)}, bf16[112,1152]{1,0:T(8,128)(2,1)S(1)}, u32[]{:S(2)}, u32[]{:S(2)}) collective-permute-start(bf16[112,1152]{1,0:T(8,128)(2,1)S(1)} %get-tuple-element.114), channel_id=1, source_target_pairs={{0,24},{4,28},{8,16},{12,20},{16,8},{20,12},{24,0},{28,4},{1,25},{... | collective-permute-start | bytes 774152 | tf_op jit(solution)/shard_map/ppermute | solution.py:670
  163.4 0.8 collective-permute-start.22
  164.3 2.4 %collective-permute-start.24 = (bf16[256,768]{1,0:T(8,128)(2,1)S(1)}, bf16[256,768]{1,0:T(8,128)(2,1)S(1)}, u32[]{:S(2)}, u32[]{:S(2)}) collective-permute-start(bf16[256,768]{1,0:T(8,128)(2,1)S(1)} %get-tuple-element.111), channel_id=1, source_target_pairs={{0,24},{4,28},{8,16},{12,20},{16,8},{20,12},{24,0},{28,4},{1,25},{... | collective-permute-start | bytes 1179656 | tf_op jit(solution)/shard_map/ppermute | solution.py:670
  166.7 1.8 collective-permute-done.18
  168.5 1.7 collective-permute-start.23
  170.2 5.0 %collective-permute-done.20 = bf16[112,1152]{1,0:T(8,128)(2,1)S(1)} collective-permute-done((bf16[112,1152]{1,0:T(8,128)(2,1)S(1)}, bf16[112,1152]{1,0:T(8,128)(2,1)S(1)}, u32[]{:S(2)}, u32[]{:S(2)}) %collective-permute-start.20) | collective-permute-done | bytes 258080 | tf_op jit(solution)/shard_map/ppermute | solution.py:670
  176.0 0.8 copy.48
  176.8 0.7 constant_dynamic-slice_fusion.6
  177.4 5.0 %collective-permute-done.22 = bf16[256,768]{1,0:T(8,128)(2,1)S(1)} collective-permute-done((bf16[256,768]{1,0:T(8,128)(2,1)S(1)}, bf16[256,768]{1,0:T(8,128)(2,1)S(1)}, u32[]{:S(2)}, u32[]{:S(2)}) %collective-permute-start.22) | collective-permute-done | bytes 393248 | tf_op jit(solution)/shard_map/ppermute | solution.py:670
  182.4 6.5 %collective-permute-done.24 = bf16[256,768]{1,0:T(8,128)(2,1)S(1)} collective-permute-done((bf16[256,768]{1,0:T(8,128)(2,1)S(1)}, bf16[256,768]{1,0:T(8,128)(2,1)S(1)}, u32[]{:S(2)}, u32[]{:S(2)}) %collective-permute-start.24) | collective-permute-done | bytes 393248 | tf_op jit(solution)/shard_map/ppermute | solution.py:670
  188.9 1.4 collective-permute-done.23
  190.5 0.8 fusion.28
  191.3 0.7 copy.46
  194.4 0.7 maximum_bitcast_fusion
  (94 shorter events, 13.0 us)
Async XLA Ops:
  6.1 1.4 collective-permute-start
  8.1 12.5 %collective-permute-start.3 = (f32[3,768]{1,0:T(4,128)S(1)}, f32[3,768]{1,0:T(4,128)S(1)}, u32[]{:S(2)}, u32[]{:S(2)}) collective-permute-start(f32[3,768]{1,0:T(4,128)S(1)} %pad_maximum_fusion.1), channel_id=1, source_target_pairs={{0,24},{4,28},{8,16},{12,20},{16,8},{20,12},{24,0},{28,4},{1,25},{... | collective-permute-start | bytes 27656 | tf_op jit(solution)/shard_map/ppermute | solution.py:670
  12.0 8.7 %collective-permute-start.2 = (f32[3,768]{1,0:T(4,128)S(1)}, f32[3,768]{1,0:T(4,128)S(1)}, u32[]{:S(2)}, u32[]{:S(2)}) collective-permute-start(f32[3,768]{1,0:T(4,128)S(1)} %pad_maximum_fusion.1), channel_id=1, source_target_pairs={{0,16},{4,20},{8,24},{12,28},{16,0},{20,4},{24,8},{28,12},{1,17},{... | collective-permute-start | bytes 27656 | tf_op jit(solution)/shard_map/ppermute | solution.py:670
  12.5 8.2 %collective-permute-start.1 = (f32[3,768]{1,0:T(4,128)S(1)}, f32[3,768]{1,0:T(4,128)S(1)}, u32[]{:S(2)}, u32[]{:S(2)}) collective-permute-start(f32[3,768]{1,0:T(4,128)S(1)} %pad_maximum_fusion.1), channel_id=1, source_target_pairs={{0,8},{4,12},{8,0},{12,4},{16,24},{20,28},{24,16},{28,20},{1,9},{5... | collective-permute-start | bytes 27656 | tf_op jit(solution)/shard_map/ppermute | solution.py:670
  21.4 17.8 %copy-start.9 = (f32[768]{0:T(1024)S(1)}, f32[768]{0:T(1024)}, u32[]{:S(2)}) copy-start(f32[768]{0:T(1024)} %param.28) | copy-start | bytes 9220
  21.4 17.8 %copy-start.10 = (f32[768]{0:T(1024)S(1)}, f32[768]{0:T(1024)}, u32[]{:S(2)}) copy-start(f32[768]{0:T(1024)} %param.29) | copy-start | bytes 9220
  21.4 17.8 %copy-start.11 = (f32[768]{0:T(1024)S(1)}, f32[768]{0:T(1024)}, u32[]{:S(2)}) copy-start(f32[768]{0:T(1024)} %param.30) | copy-start | bytes 9220
  21.4 17.9 %copy-start.12 = (f32[768]{0:T(1024)S(1)}, f32[768]{0:T(1024)}, u32[]{:S(2)}) copy-start(f32[768]{0:T(1024)} %param.34) | copy-start | bytes 9220
  21.4 17.9 %copy-start.13 = (f32[768]{0:T(1024)S(1)}, f32[768]{0:T(1024)}, u32[]{:S(2)}) copy-start(f32[768]{0:T(1024)} %param.35) | copy-start | bytes 9220
  21.4 17.9 %copy-start.14 = (f32[768]{0:T(1024)S(1)}, f32[768]{0:T(1024)}, u32[]{:S(2)}) copy-start(f32[768]{0:T(1024)} %param.36) | copy-start | bytes 9220
  21.4 17.9 %copy-start.8 = (f32[3072]{0:T(1024)S(1)}, f32[3072]{0:T(1024)}, u32[]{:S(2)}) copy-start(f32[3072]{0:T(1024)} %param.32) | copy-start | bytes 36868
  34.1 14.8 %collective-permute-start.6 = (bf16[512,384]{1,0:T(8,128)(2,1)}, bf16[512,384]{1,0:T(8,128)(2,1)S(1)}, u32[]{:S(2)}, u32[]{:S(2)}) collective-permute-start(bf16[512,384]{1,0:T(8,128)(2,1)} %get-tuple-element.41.refs_2_.heads_ref), channel_id=1, source_target_pairs={{0,3},{1,2},{2,1},{3,0},{4,7},{5,6},{6,5},{7,4},{8,11},{9,10},{10,... | collective-permute-start | bytes 1179656 | tf_op jit(solution)/shard_map/ppermute | solution.py:670
  38.5 33.1 %collective-permute-start.5 = (bf16[512,384]{1,0:T(8,128)(2,1)}, bf16[512,384]{1,0:T(8,128)(2,1)S(1)}, u32[]{:S(2)}, u32[]{:S(2)}) collective-permute-start(bf16[512,384]{1,0:T(8,128)(2,1)} %get-tuple-element.41.refs_2_.heads_ref), channel_id=1, source_target_pairs={{0,2},{1,3},{2,0},{3,1},{4,6},{5,7},{6,4},{7,5},{8,10},{9,11},{10,... | collective-permute-start | bytes 1179656 | tf_op jit(solution)/shard_map/ppermute | solution.py:670
  38.5 33.1 %collective-permute-start.4 = (bf16[512,384]{1,0:T(8,128)(2,1)}, bf16[512,384]{1,0:T(8,128)(2,1)S(1)}, u32[]{:S(2)}, u32[]{:S(2)}) collective-permute-start(bf16[512,384]{1,0:T(8,128)(2,1)} %get-tuple-element.41.refs_2_.heads_ref), channel_id=1, source_target_pairs={{0,1},{1,0},{2,3},{3,2},{4,5},{5,4},{6,7},{7,6},{8,9},{9,8},{10,11... | collective-permute-start | bytes 1179656 | tf_op jit(solution)/shard_map/ppermute | solution.py:670
  48.9 22.8 %copy-start.3 = (bf16[512,384]{1,0:T(8,128)(2,1)}, bf16[512,384]{1,0:T(8,128)(2,1)S(1)}, u32[]{:S(2)}) copy-start(bf16[512,384]{1,0:T(8,128)(2,1)S(1)} %collective-permute-done.6.refs_5_) | copy-start | bytes 1179652
  71.6 0.7 copy-start.4
  72.4 0.7 copy-start.5
  120.9 35.2 %copy-start.2 = (f32[128,768]{1,0:T(8,128)S(1)}, f32[128,768]{1,0:T(8,128)}, u32[]{:S(2)}) copy-start(f32[128,768]{1,0:T(8,128)} %get-tuple-element.43) | copy-start | bytes 1179652
  120.9 35.2 %copy-start.7 = (f32[768]{0:T(1024)S(1)}, f32[768]{0:T(1024)}, u32[]{:S(2)}) copy-start(f32[768]{0:T(1024)} %param.37) | copy-start | bytes 9220
  121.7 5.8 %collective-permute-start.10 = (f32[2,768]{1,0:T(2,128)S(1)}, f32[2,768]{1,0:T(2,128)S(1)}, u32[]{:S(2)}, u32[]{:S(2)}) collective-permute-start(f32[2,768]{1,0:T(2,128)S(1)} %slice.153), channel_id=1, source_target_pairs={{0,4},{4,0},{8,12},{12,8},{16,20},{20,16},{24,28},{28,24},{1,5},{5... | collective-permute-start | bytes 18440 | tf_op jit(solution)/shard_map/ppermute | solution.py:670
  127.0 32.0 %copy-start.1 = (f32[4,112,1152]{2,1,0:T(8,128)S(1)}, f32[4,112,1152]{2,1,0:T(8,128)}, u32[]{:S(2)}) copy-start(f32[4,112,1152]{2,1,0:T(8,128)} %get-tuple-element.57) | copy-start | bytes 6193156
  127.0 32.0 %collective-permute-start.17 = (bf16[4,112,1152]{2,1,0:T(8,128)(2,1)}, bf16[4,112,1152]{2,1,0:T(8,128)(2,1)S(1)}, u32[]{:S(2)}, u32[]{:S(2)}) collective-permute-start(bf16[4,112,1152]{2,1,0:T(8,128)(2,1)} %get-tuple-element.58), channel_id=1, source_target_pairs={{0,4},{4,0},{8,12},{12,8},{16,20},{20,16},{24,28},{28,24},{1,5},{5... | collective-permute-start | bytes 3096584 | tf_op jit(solution)/shard_map/ppermute | solution.py:670
  128.3 4.5 %collective-permute-start.13 = (f32[2,768]{1,0:T(2,128)S(1)}, f32[2,768]{1,0:T(2,128)S(1)}, u32[]{:S(2)}, u32[]{:S(2)}) collective-permute-start(f32[2,768]{1,0:T(2,128)S(1)} %slice_add_fusion.6), channel_id=1, source_target_pairs={{0,24},{4,28},{8,16},{12,20},{16,8},{20,12},{24,0},{28,4},{1,25},{... | collective-permute-start | bytes 18440 | tf_op jit(solution)/shard_map/ppermute | solution.py:670
  130.8 3.6 %collective-permute-start.12 = (f32[2,768]{1,0:T(2,128)S(1)}, f32[2,768]{1,0:T(2,128)S(1)}, u32[]{:S(2)}, u32[]{:S(2)}) collective-permute-start(f32[2,768]{1,0:T(2,128)S(1)} %slice_add_fusion.6), channel_id=1, source_target_pairs={{0,16},{4,20},{8,24},{12,28},{16,0},{20,4},{24,8},{28,12},{1,17},{... | collective-permute-start | bytes 18440 | tf_op jit(solution)/shard_map/ppermute | solution.py:670
  131.3 3.6 %collective-permute-start.11 = (f32[2,768]{1,0:T(2,128)S(1)}, f32[2,768]{1,0:T(2,128)S(1)}, u32[]{:S(2)}, u32[]{:S(2)}) collective-permute-start(f32[2,768]{1,0:T(2,128)S(1)} %slice_add_fusion.6), channel_id=1, source_target_pairs={{0,8},{4,12},{8,0},{12,4},{16,24},{20,28},{24,16},{28,20},{1,9},{5... | collective-permute-start | bytes 18440 | tf_op jit(solution)/shard_map/ppermute | solution.py:670
  134.9 6.3 %collective-permute-start.16 = (f32[2,768]{1,0:T(2,128)S(1)}, f32[2,768]{1,0:T(2,128)S(1)}, u32[]{:S(2)}, u32[]{:S(2)}) collective-permute-start(f32[2,768]{1,0:T(2,128)S(1)} %add_add_fusion.1), channel_id=1, source_target_pairs={{0,3},{1,2},{2,1},{3,0},{4,7},{5,6},{6,5},{7,4},{8,11},{9,10},{10,... | collective-permute-start | bytes 18440 | tf_op jit(solution)/shard_map/ppermute | solution.py:670
  137.6 9.3 %collective-permute-start.15 = (f32[2,768]{1,0:T(2,128)S(1)}, f32[2,768]{1,0:T(2,128)S(1)}, u32[]{:S(2)}, u32[]{:S(2)}) collective-permute-start(f32[2,768]{1,0:T(2,128)S(1)} %add_add_fusion.1), channel_id=1, source_target_pairs={{0,2},{1,3},{2,0},{3,1},{4,6},{5,7},{6,4},{7,5},{8,10},{9,11},{10,... | collective-permute-start | bytes 18440 | tf_op jit(solution)/shard_map/ppermute | solution.py:670
  137.6 9.3 %collective-permute-start.14 = (f32[2,768]{1,0:T(2,128)S(1)}, f32[2,768]{1,0:T(2,128)S(1)}, u32[]{:S(2)}, u32[]{:S(2)}) collective-permute-start(f32[2,768]{1,0:T(2,128)S(1)} %add_add_fusion.1), channel_id=1, source_target_pairs={{0,1},{1,0},{2,3},{3,2},{4,5},{5,4},{6,7},{7,6},{8,9},{9,8},{10,11... | collective-permute-start | bytes 18440 | tf_op jit(solution)/shard_map/ppermute | solution.py:670
  140.0 14.2 %collective-permute-start.7 = (bf16[128,768]{1,0:T(8,128)(2,1)}, bf16[128,768]{1,0:T(8,128)(2,1)S(1)}, u32[]{:S(2)}, u32[]{:S(2)}) collective-permute-start(bf16[128,768]{1,0:T(8,128)(2,1)} %get-tuple-element.49), channel_id=1, source_target_pairs={{0,2},{1,3},{2,0},{3,1},{4,6},{5,7},{6,4},{7,5},{8,10},{9,11},{10,... | collective-permute-start | bytes 589832 | tf_op jit(solution)/shard_map/ppermute | solution.py:670
  141.2 12.9 %collective-permute-start.8 = (bf16[128,768]{1,0:T(8,128)(2,1)}, bf16[128,768]{1,0:T(8,128)(2,1)S(1)}, u32[]{:S(2)}, u32[]{:S(2)}) collective-permute-start(bf16[128,768]{1,0:T(8,128)(2,1)} %get-tuple-element.50), channel_id=1, source_target_pairs={{0,3},{1,2},{2,1},{3,0},{4,7},{5,6},{6,5},{7,4},{8,11},{9,10},{10,... | collective-permute-start | bytes 589832 | tf_op jit(solution)/shard_map/ppermute | solution.py:670
  147.0 9.1 %collective-permute-start.9 = (bf16[128,768]{1,0:T(8,128)(2,1)}, bf16[128,768]{1,0:T(8,128)(2,1)S(1)}, u32[]{:S(2)}, u32[]{:S(2)}) collective-permute-start(bf16[128,768]{1,0:T(8,128)(2,1)} %get-tuple-element.52), channel_id=1, source_target_pairs={{0,1},{1,0},{2,3},{3,2},{4,5},{5,4},{6,7},{7,6},{8,9},{9,8},{10,11... | collective-permute-start | bytes 589832 | tf_op jit(solution)/shard_map/ppermute | solution.py:670
  147.0 15.8 %collective-permute-start.21 = (bf16[4,256,768]{2,1,0:T(8,128)(2,1)}, bf16[4,256,768]{2,1,0:T(8,128)(2,1)S(1)}, u32[]{:S(2)}, u32[]{:S(2)}) collective-permute-start(bf16[4,256,768]{2,1,0:T(8,128)(2,1)} %get-tuple-element.60), channel_id=1, source_target_pairs={{0,4},{4,0},{8,12},{12,8},{16,20},{20,16},{24,28},{28,24},{1,5},{5... | collective-permute-start | bytes 4718600 | tf_op jit(solution)/shard_map/ppermute | solution.py:670
  148.3 10.9 %copy-start.6 = (f32[768]{0:T(1024)}, f32[768]{0:T(1024)S(1)}, u32[]{:S(2)}) copy-start(f32[768]{0:T(1024)S(1)} %get-tuple-element.96) | copy-start | bytes 9220
  158.9 3.9 %copy-start = (f32[4,256,768]{2,1,0:T(8,128)S(1)}, f32[4,256,768]{2,1,0:T(8,128)}, u32[]{:S(2)}) copy-start(f32[4,256,768]{2,1,0:T(8,128)} %get-tuple-element.59) | copy-start | bytes 9437188
  159.2 9.2 %collective-permute-start.18 = (bf16[112,1152]{1,0:T(8,128)(2,1)S(1)}, bf16[112,1152]{1,0:T(8,128)(2,1)S(1)}, u32[]{:S(2)}, u32[]{:S(2)}) collective-permute-start(bf16[112,1152]{1,0:T(8,128)(2,1)S(1)} %get-tuple-element.113), channel_id=1, source_target_pairs={{0,8},{4,12},{8,0},{12,4},{16,24},{20,28},{24,16},{28,20},{1,9},{5... | collective-permute-start | bytes 774152 | tf_op jit(solution)/shard_map/ppermute | solution.py:670
  160.1 15.1 %collective-permute-start.20 = (bf16[112,1152]{1,0:T(8,128)(2,1)S(1)}, bf16[112,1152]{1,0:T(8,128)(2,1)S(1)}, u32[]{:S(2)}, u32[]{:S(2)}) collective-permute-start(bf16[112,1152]{1,0:T(8,128)(2,1)S(1)} %get-tuple-element.114), channel_id=1, source_target_pairs={{0,24},{4,28},{8,16},{12,20},{16,8},{20,12},{24,0},{28,4},{1,25},{... | collective-permute-start | bytes 774152 | tf_op jit(solution)/shard_map/ppermute | solution.py:670
  162.5 13.3 %collective-permute-start.19 = (bf16[112,1152]{1,0:T(8,128)(2,1)S(1)}, bf16[112,1152]{1,0:T(8,128)(2,1)S(1)}, u32[]{:S(2)}, u32[]{:S(2)}) collective-permute-start(bf16[112,1152]{1,0:T(8,128)(2,1)S(1)} %get-tuple-element.115), channel_id=1, source_target_pairs={{0,16},{4,20},{8,24},{12,28},{16,0},{20,4},{24,8},{28,12},{1,17},{... | collective-permute-start | bytes 774152 | tf_op jit(solution)/shard_map/ppermute | solution.py:670
  163.4 19.0 %collective-permute-start.22 = (bf16[256,768]{1,0:T(8,128)(2,1)S(1)}, bf16[256,768]{1,0:T(8,128)(2,1)S(1)}, u32[]{:S(2)}, u32[]{:S(2)}) collective-permute-start(bf16[256,768]{1,0:T(8,128)(2,1)S(1)} %get-tuple-element.110), channel_id=1, source_target_pairs={{0,8},{4,12},{8,0},{12,4},{16,24},{20,28},{24,16},{28,20},{1,9},{5... | collective-permute-start | bytes 1179656 | tf_op jit(solution)/shard_map/ppermute | solution.py:670
  164.3 24.7 %collective-permute-start.24 = (bf16[256,768]{1,0:T(8,128)(2,1)S(1)}, bf16[256,768]{1,0:T(8,128)(2,1)S(1)}, u32[]{:S(2)}, u32[]{:S(2)}) collective-permute-start(bf16[256,768]{1,0:T(8,128)(2,1)S(1)} %get-tuple-element.111), channel_id=1, source_target_pairs={{0,24},{4,28},{8,16},{12,20},{16,8},{20,12},{24,0},{28,4},{1,25},{... | collective-permute-start | bytes 1179656 | tf_op jit(solution)/shard_map/ppermute | solution.py:670
  168.5 21.8 %collective-permute-start.23 = (bf16[256,768]{1,0:T(8,128)(2,1)S(1)}, bf16[256,768]{1,0:T(8,128)(2,1)S(1)}, u32[]{:S(2)}, u32[]{:S(2)}) collective-permute-start(bf16[256,768]{1,0:T(8,128)(2,1)S(1)} %get-tuple-element.112), channel_id=1, source_target_pairs={{0,16},{4,20},{8,24},{12,28},{16,0},{20,4},{24,8},{28,12},{1,17},{... | collective-permute-start | bytes 1179656 | tf_op jit(solution)/shard_map/ppermute | solution.py:670
